TPU v7x, 128 devices: a whole 4x4x4 slice. The times are simulated.
128 devices in a mesh: rows: 32 (over x, y, z_lo), seq: 4 (over z_hi, core).
Axes of the slice: x: 4, y: 4, z: 4 (z_hi: 2, z_lo: 2; z = z_hi * 2 + z_lo), core: 2. Of those that a mesh axis runs over, the one named last changes fastest.
Arguments:
- image: bfloat16 [256, 256, 256], P('rows', 'seq'), may hold values from -42 to 42
- gain_attn: float32 [256], replicated, may hold values from 0.1 to 1.9
- w_qkv_fine: bfloat16 [256, 768], replicated, may hold values from -0.375 to 0.375
- scale_fine: float32 [4], replicated, may hold values from 8 to 40
- w_out_fine: bfloat16 [256, 256], replicated, may hold values from -1.5 to 1.5
- gain_ffn: float32 [256], replicated, may hold values from 0.1 to 1.9
- w_ffn_in: bfloat16 [256, 1536], replicated, may hold values from -0.375 to 0.375
- w_ffn_out: bfloat16 [768, 256], replicated, may hold values from -0.4375 to 0.4375
- w_merge: bfloat16 [1024, 1024], replicated, may hold values from -0.1875 to 0.1875
- gain_coarse: float32 [1024], replicated, may hold values from 0.1 to 1.9
- w_qkv_coarse: bfloat16 [1024, 3072], replicated, may hold values from -0.1875 to 0.1875
- scale_coarse: float32 [16], replicated, may hold values from 24 to 48
- w_out_coarse: bfloat16 [1024, 1024], replicated, may hold values from -0.75 to 0.75
Outputs:
- fine_out: bfloat16 [256, 256, 256], P('rows', 'seq')
- coarse_out: bfloat16 [128, 128, 1024], P('rows', 'seq')
All inputs are finite; a program needn't handle non-finite values.
Results may differ from a plain program's by a relative error of at most 0.025.
The roundings to bfloat16 on the way count: a program that leaves them out, or rounds other values in their place, can miss the bound.
Values may be sent and summed in bfloat16 or wider, within the bound.
A program may use at most 128 MiB of HBM per device.

v0:
```python
import math

import jax
import jax.numpy as jnp
from jax import lax
from jax.sharding import PartitionSpec as P

HEAD = 64


def extended(array, sides, width):
    for axis, dim in sides:
        count, length = (lax.axis_size(axis), array.shape[dim])
        up = [(i, (i + 1) % count) for i in range(count - 1)]
        down = [(j, i) for i, j in up]
        last = lax.slice_in_dim(array, length - width, length, axis=dim)
        leading = lax.slice_in_dim(array, 0, width, axis=dim)
        before = lax.ppermute(last, axis, up)
        after = lax.ppermute(leading, axis, down)
        array = jnp.concatenate([before, array, after], axis=dim)
    return array


def rms_scaled(values, gain):
    mean_square = jnp.mean(values * values, axis=-1, keepdims=True)
    return values * lax.rsqrt(mean_square + 1e-06) * gain


def unit_heads(values, head_count):
    shaped = values.astype(jnp.float32).reshape(values.shape[:-1] + (head_count, HEAD))
    mean_square = jnp.mean(shaped * shaped, axis=-1, keepdims=True)
    return (shaped * lax.rsqrt(mean_square + 1e-06)).astype(jnp.bfloat16)


def window_tiles(padded, row_count, col_count):
    bands = jnp.stack(
        [padded[start_row : start_row + row_count : 4] for start_row in range(10)], axis=0
    )
    return jnp.stack(
        [bands[:, :, start_col : start_col + col_count : 16] for start_col in range(22)], axis=1
    )


def neighbour_attention(projected, padded_pairs, scale_fine):
    row_count, col_count, triple = projected.shape
    width = triple // 3
    head_count = width // HEAD
    tile_rows = row_count // 4
    tile_cols = col_count // 16
    queries = unit_heads(projected[:, :, :width], head_count)
    queries = queries.reshape(tile_rows, 4, tile_cols, 16, head_count, HEAD)
    queries = queries.transpose(0, 2, 4, 1, 3, 5).reshape(
        tile_rows, tile_cols, head_count, 64, HEAD
    )
    padded_unit = unit_heads(padded_pairs[:, :, :width], head_count).reshape(
        row_count + 6, col_count + 6, width
    )
    joined = jnp.concatenate([padded_unit, padded_pairs[:, :, width:]], axis=-1)
    tiles = window_tiles(joined, row_count, col_count).reshape(
        220, tile_rows, tile_cols, 2, head_count, HEAD
    )
    key_tiles = tiles[:, :, :, 0].transpose(1, 2, 3, 0, 4)
    value_tiles = tiles[:, :, :, 1].transpose(1, 2, 3, 0, 4)
    query_row = jnp.arange(64) // 16
    query_col = jnp.arange(64) % 16
    key_row = jnp.arange(220) // 22
    key_col = jnp.arange(220) % 22
    row_gap = key_row[None, :] - query_row[:, None]
    col_gap = key_col[None, :] - query_col[:, None]
    nearby = (row_gap >= 0) & (row_gap <= 6) & (col_gap >= 0) & (col_gap <= 6)
    first_row = lax.axis_index("rows") * row_count
    first_col = lax.axis_index("seq") * col_count
    global_row = first_row + 4 * jnp.arange(tile_rows)[:, None] + key_row[None, :] - 3
    global_col = first_col + 16 * jnp.arange(tile_cols)[:, None] + key_col[None, :] - 3
    row_inside = (global_row >= 0) & (global_row < row_count * lax.axis_size("rows"))
    col_inside = (global_col >= 0) & (global_col < col_count * lax.axis_size("seq"))
    allowed = (
        nearby[None, None, None]
        & row_inside[:, None, None, None, :]
        & col_inside[None, :, None, None, :]
    )
    factor = scale_fine / HEAD
    scores = (
        jnp.einsum("ijhqe,ijhke->ijhqk", queries, key_tiles, preferred_element_type=jnp.float32)
        * factor[None, None, :, None, None]
    )
    weights = jnp.where(allowed, jnp.exp(scores), 0.0)
    denominator = jnp.sum(weights, axis=-1)
    numerator = jnp.einsum(
        "ijhqk,ijhke->ijhqe",
        weights.astype(jnp.bfloat16),
        value_tiles,
        preferred_element_type=jnp.float32,
    )
    attended = (numerator / denominator[..., None]).astype(jnp.bfloat16)
    attended = attended.reshape(tile_rows, tile_cols, head_count, 4, 16, HEAD).transpose(
        0, 3, 1, 4, 2, 5
    )
    return attended.reshape(row_count, col_count, width)


def fold_keys(queries, factor, partial_sums, pieces):
    group_heads = factor.shape[0]
    key_part, value_part = pieces
    key_count = key_part.shape[0]
    block_size = math.gcd(key_count, 512)
    key_blocks = key_part.reshape(key_count // block_size, block_size, group_heads, HEAD)
    value_blocks = value_part.reshape(key_count // block_size, block_size, group_heads, HEAD)

    def block_step(running, blocks):
        totals, weight_sum = running
        key_block, value_block = blocks
        scores = (
            jnp.einsum("qhe,khe->hqk", queries, key_block, preferred_element_type=jnp.float32)
            * factor[:, None, None]
        )
        weights = jnp.exp(scores)
        weight_sum = weight_sum + jnp.sum(weights, axis=-1)
        update = jnp.einsum(
            "hqk,khe->qhe",
            weights.astype(jnp.bfloat16),
            value_block,
            preferred_element_type=jnp.float32,
        )
        return ((totals + update.reshape(totals.shape), weight_sum), None)

    result, unused = lax.scan(block_step, partial_sums, (key_blocks, value_blocks))
    return result


def body(
    image,
    gain_attn,
    w_qkv_fine,
    scale_fine,
    w_out_fine,
    gain_ffn,
    w_ffn_in,
    w_ffn_out,
    w_merge,
    gain_coarse,
    w_qkv_coarse,
    scale_coarse,
    w_out_coarse,
):
    row_count, col_count, width = image.shape
    stream = image.astype(jnp.float32)
    normed = rms_scaled(stream, gain_attn).astype(jnp.bfloat16)
    projected = jnp.dot(
        normed.reshape(-1, width), w_qkv_fine, preferred_element_type=jnp.float32
    ).astype(jnp.bfloat16)
    projected = projected.reshape(row_count, col_count, 3 * width)
    padded_pairs = extended(projected[:, :, width:], (("rows", 0), ("seq", 1)), 3)
    attended = neighbour_attention(projected, padded_pairs, scale_fine)
    stream = stream.reshape(-1, width) + jnp.dot(
        attended.reshape(-1, width), w_out_fine, preferred_element_type=jnp.float32
    )
    hidden_units = w_ffn_out.shape[0]
    normed_ffn = rms_scaled(stream, gain_ffn).astype(jnp.bfloat16)
    mixed = jnp.dot(normed_ffn, w_ffn_in, preferred_element_type=jnp.float32)
    gated = (mixed[:, :hidden_units] * jax.nn.gelu(mixed[:, hidden_units:])).astype(jnp.bfloat16)
    fine_out = (stream + jnp.dot(gated, w_ffn_out, preferred_element_type=jnp.float32)).astype(
        jnp.bfloat16
    )
    fine_out = fine_out.reshape(row_count, col_count, width)
    merged = (
        fine_out.reshape(row_count // 2, 2, col_count // 2, 2, width)
        .transpose(0, 2, 1, 3, 4)
        .reshape(-1, 4 * width)
    )
    coarse_in = jnp.dot(merged, w_merge, preferred_element_type=jnp.float32).astype(jnp.bfloat16)
    token_count, coarse_width = coarse_in.shape
    head_total = coarse_width // HEAD
    groups = lax.axis_size("seq")
    group_heads = head_total // groups
    coarse_stream = coarse_in.astype(jnp.float32)
    normed_coarse = rms_scaled(coarse_stream, gain_coarse).astype(jnp.bfloat16)
    triple = jnp.dot(normed_coarse, w_qkv_coarse, preferred_element_type=jnp.float32).astype(
        jnp.bfloat16
    )
    query_unit = unit_heads(triple[:, :coarse_width], head_total).reshape(token_count, coarse_width)
    key_unit = unit_heads(triple[:, coarse_width : 2 * coarse_width], head_total).reshape(
        token_count, coarse_width
    )
    value_part = triple[:, 2 * coarse_width :]
    factor = (
        lax.dynamic_slice_in_dim(scale_coarse, lax.axis_index("seq") * group_heads, group_heads)
        / HEAD
    )
    query_count = groups * token_count
    initial = (
        jnp.zeros((query_count, group_heads * HEAD), jnp.float32),
        jnp.zeros((group_heads, query_count), jnp.float32),
    )
    stacked = jnp.stack([query_unit, key_unit, value_part], axis=1).reshape(
        token_count, 3, groups, group_heads * HEAD
    )
    moved = lax.all_to_all(stacked, "seq", split_axis=2, concat_axis=0, tiled=True)
    queries = moved[:, 0, 0].reshape(query_count, group_heads, HEAD)
    totals, weight_sum = fold_keys(
        queries,
        factor,
        initial,
        (
            lax.all_gather(moved[:, 1, 0], "rows", axis=0, tiled=True),
            lax.all_gather(moved[:, 2, 0], "rows", axis=0, tiled=True),
        ),
    )
    attended_coarse = totals.reshape(query_count, group_heads, HEAD) / weight_sum.T[:, :, None]
    attended_coarse = attended_coarse.astype(jnp.bfloat16).reshape(
        query_count, 1, group_heads * HEAD
    )
    returned = lax.all_to_all(
        attended_coarse, "seq", split_axis=0, concat_axis=1, tiled=True
    ).reshape(token_count, coarse_width)
    coarse_out = (
        coarse_stream + jnp.dot(returned, w_out_coarse, preferred_element_type=jnp.float32)
    ).astype(jnp.bfloat16)
    return (fine_out, coarse_out.reshape(row_count // 2, col_count // 2, coarse_width))


def solution(mesh):
    placed = (P("rows", "seq", None), P(), P(), P(), P(), P(), P(), P(), P(), P(), P(), P(), P())
    return jax.shard_map(
        body,
        mesh=mesh,
        in_specs=placed,
        out_specs=(P("rows", "seq", None), P("rows", "seq", None)),
        check_vma=False,
    )
```

profile of v0, /device:TPU:1, one launch (start us, length us, event | category | flops | bytes accessed | tf_op | source)
XLA Modules:
  0.0 816.1 jit_solution(10387814739758997745)
XLA Ops:
  11.7 5.0 collective-permute-start
  28.9 6.1 collective-permute-start.2
  66.8 6.2 slice.170
  73.0 6.2 slice.171
  79.2 6.2 slice.172
  85.4 6.2 slice.173
  91.5 6.2 slice.174
  97.7 4.9 slice.175
  102.6 4.9 slice.176
  107.4 4.9 slice.177
  112.3 4.8 slice.178
  117.2 4.8 slice.179
  122.0 4.8 slice.180
  126.9 4.8 slice.181
  131.8 4.8 slice.182
  136.6 4.8 slice.183
  141.5 4.8 slice.184
  146.3 4.8 slice.185
  151.2 4.8 slice.186
  160.8 4.8 slice.188
  165.6 4.8 slice.189
  187.4 6.9 reshape.383
  194.3 5.1 fusion.56
  222.3 13.7 %all_to_all.33 = bf16[128,3,4,256]{0,3,1,2:T(8,128)(2,1)S(1)} all-to-all(bf16[128,3,4,256]{0,3,1,2:T(8,128)(2,1)S(1)} %copy.142), channel_id=1, replica_groups=mesh['rows'=32,'seq'=4] {'seq'}, dimensions={2} | all-to-all | bytes 1572864 | tf_op jit(solution)/shard_map/all_to_all | solution.py:198
  238.1 187.8 %all-gather.5.cloned.1.call-done = bf16[16384,1,1,256]{3,0,1,2:T(8,128)(2,1)} async-done(((bf16[512,1,1,256]{3,0,1,2:T(8,128)(2,1)}), bf16[16384,1,1,256]{3,0,1,2:T(8,128)(2,1)}) %all-gather.5.cloned.1.call-update) | async-done | bytes 8388624 | tf_op jit(solution)/shard_map/all_gather | solution.py:206
  426.0 24.5 %reshape.398 = bf16[32,512,4,64]{3,2,1,0:T(4,128)(2,1)} reshape(bf16[16384,1,1,256]{3,0,1,2:T(8,128)(2,1)} %all-gather.5.cloned.1.call-done) | data formatting | bytes 16777216 | tf_op jit(solution)/shard_map/reshape | solution.py:108
  450.5 24.3 %copy.147 = bf16[32,512,4,64]{1,3,2,0:T(8,128)(2,1)} copy(bf16[32,512,4,64]{3,2,1,0:T(4,128)(2,1)} %reshape.398) | data formatting | bytes 16777216
  474.8 142.1 %all-gather.7.cloned.1.call-done = bf16[16384,1,1,256]{3,0,1,2:T(8,128)(2,1)} async-done(((bf16[512,1,1,256]{3,0,1,2:T(8,128)(2,1)}), bf16[16384,1,1,256]{3,0,1,2:T(8,128)(2,1)}) %all-gather.7.cloned.1.call-update) | async-done | bytes 8388624 | tf_op jit(solution)/shard_map/all_gather | solution.py:205
  616.8 24.5 %reshape.399 = bf16[32,512,4,64]{3,2,1,0:T(4,128)(2,1)} reshape(bf16[16384,1,1,256]{3,0,1,2:T(8,128)(2,1)} %all-gather.7.cloned.1.call-done) | data formatting | bytes 16777216 | tf_op jit(solution)/shard_map/reshape | solution.py:107
  641.3 24.2 %copy.148 = bf16[32,512,4,64]{1,3,2,0:T(8,128)(2,1)} copy(bf16[32,512,4,64]{3,2,1,0:T(4,128)(2,1)} %reshape.399) | data formatting | bytes 16777216
  665.5 126.2 %while.13 = (s32[]{:T(128)}, f32[512,256]{0,1:T(8,128)S(1)}, f32[4,512]{1,0:T(4,128)S(1)}, bf16[32,512,4,64]{1,3,2,0:T(8,128)(2,1)}, bf16[32,512,4,64]{1,3,2,0:T...) while((s32[]{:T(128)}, f32[512,256]{0,1:T(8,128)S(1)}, ...), condition=%wide.region_10.11_spmd.clone, body=%wide.region_8.10_spmd.clone.sunk | while | flops 272893952 | bytes 11306120 | solution.py:127
  793.3 12.5 %all_to_all.34 = bf16[4,2,16384]{2,1,0:T(2,128)(2,1)S(1)} all-to-all(bf16[4,2,16384]{2,1,0:T(2,128)(2,1)S(1)} %reshape.400), channel_id=1, replica_groups=mesh['rows'=32,'seq'=4] {'seq'}, dimensions={0} | all-to-all | bytes 524288 | tf_op jit(solution)/shard_map/all_to_all | solution.py:213
  (285 shorter events, 224.8 us)
Async XLA Ops:
  7.2 207.2 %copy-start = (bf16[1024,1024]{1,0:T(8,128)(2,1)S(1)}, bf16[1024,1024]{1,0:T(8,128)(2,1)}, u32[]{:S(2)}) copy-start(bf16[1024,1024]{1,0:T(8,128)(2,1)} %param.23) | copy-start | bytes 6291460
  7.2 418.8 %all-gather.5.cloned.1.call-start = ((), (), s32[]{:S(2)}) async-start(), calls=%async_computation.2 | async-start | bytes 8650752 | tf_op jit(solution)/shard_map/all_gather | solution.py:206
  11.7 16.3 %collective-permute-start = (bf16[3,64,512]{2,1,0:T(8,128)(2,1)}, bf16[3,64,512]{2,1,0:T(8,128)(2,1)}, u32[]{:S(2)}, u32[]{:S(2)}) collective-permute-start(bf16[3,64,512]{2,1,0:T(8,128)(2,1)} %get-tuple-element.136), channel_id=1, source_target_pairs={{0,4},{4,8},{8,12},{12,16},{16,20},{20,24},{24,28},{28,32},{32,36}... | collective-permute-start | bytes 589832 | tf_op jit(solution)/shard_map/ppermute | solution.py:18
  16.8 11.3 %collective-permute-start.1 = (bf16[3,64,512]{2,1,0:T(8,128)(2,1)}, bf16[3,64,512]{2,1,0:T(8,128)(2,1)}, u32[]{:S(2)}, u32[]{:S(2)}) collective-permute-start(bf16[3,64,512]{2,1,0:T(8,128)(2,1)} %get-tuple-element.137), channel_id=1, source_target_pairs={{4,0},{8,4},{12,8},{16,12},{20,16},{24,20},{28,24},{32,28},{36,32}... | collective-permute-start | bytes 589832 | tf_op jit(solution)/shard_map/ppermute | solution.py:19
  18.1 9.9 %copy-start.2 = (bf16[8,64,512]{2,1,0:T(8,128)(2,1)}, bf16[8,64,512]{2,1,0:T(8,128)(2,1)S(1)}, u32[]{:S(2)}) copy-start(bf16[8,64,512]{2,1,0:T(8,128)(2,1)S(1)} %slice.204) | copy-start | bytes 1572868
  25.3 11.8 %copy-start.11 = (f32[4]{0:T(128)S(1)}, f32[4]{0:T(128)}, u32[]{:S(2)}) copy-start(f32[4]{0:T(128)} %param.18) | copy-start | bytes 52
  28.9 9.1 %collective-permute-start.2 = (bf16[14,3,512]{2,1,0:T(4,128)(2,1)S(1)}, bf16[14,3,512]{2,1,0:T(4,128)(2,1)S(1)}, u32[]{:S(2)}, u32[]{:S(2)}) collective-permute-start(bf16[14,3,512]{2,1,0:T(4,128)(2,1)S(1)} %get-tuple-element.126), channel_id=1, source_target_pairs={{0,1},{1,2},{2,3},{4,5},{5,6},{6,7},{8,9},{9,10},{10,11},{12,13},{... | collective-permute-start | bytes 129032 | tf_op jit(solution)/shard_map/ppermute | solution.py:18
  34.9 7.0 collective-permute-start.3
  58.7 1.4 copy-start.4
  203.4 3.2 copy-start.7
  209.3 1.0 copy-start.3
  209.3 1.0 copy-start.6
  209.3 1.3 copy-start.9
  210.6 1.8 copy-start.10
  213.2 0.7 copy-start.5
  214.2 0.7 copy-start.8
  236.0 1.9 copy-start.12
  237.1 379.7 %all-gather.7.cloned.1.call-start = ((), (), s32[]{:S(2)}) async-start(), calls=%async_computation.3 | async-start | bytes 8650752 | tf_op jit(solution)/shard_map/all_gather | solution.py:205
  806.2 3.1 copy-start.1
Sparse Core Ops, SparseCore 0:
  237.2 188.6 all-gather.4
  428.2 188.5 all-gather.6
where the time goes:
time: 824 us; the launch traced here: 816 us
  waiting for transfers between devices  335 us (41%)
  local copies, waits for them, and re-layouts  266 us (32%)
  matrix products  134 us (16%)
  blocking collectives  26.2 us (3%)
  other arithmetic  25.3 us (3%)
  between operations  14.9 us (2%)
  starting transfers between devices  14.6 us (2%)
    all_gather x1, waiting for transfers between devices, body(): lax.all_gather(moved[:, 2, 0], 'rows', axis=0, tiled=True)  188 us
    all_gather x1, waiting for transfers between devices, body(): lax.all_gather(moved[:, 1, 0], 'rows', axis=0, tiled=True)  142 us
    slice x22, local copies, waits for them, and re-layouts, window_tiles(): bands[:, :, start_col:start_col + col_count:16]  113 us
    unnamed x64, local copies, waits for them, and re-layouts  68.4 us
    dot_general x32, matrix products, block_step(): jnp.einsum('qhe,khe->hqk', queries, key_block, preferred_element_type=jnp...  62.1 us
    dot_general x32, matrix products, block_step(): jnp.einsum('hqk,khe->qhe', weights.astype(jnp.bfloat16), value_block, pre...  57.5 us
    reshape x1, local copies, waits for them, and re-layouts, fold_keys(): value_part.reshape(key_count // block_size, block_size, group_heads, HEAD)  24.5 us
    reshape x1, local copies, waits for them, and re-layouts, fold_keys(): key_part.reshape(key_count // block_size, block_size, group_heads, HEAD)  24.5 us
  transfers between devices with their start and end apart: 6, of which 3 were waited for; matrix products, arithmetic and copies ran while one was open for 7% of the time, Pallas kernels for 0%

commit v1 on v0

v1 whole, which is shorter than its diff:
```python
import functools
import math

import jax
import jax.numpy as jnp
from jax import lax
from jax.experimental import pallas as pl
from jax.experimental.pallas import tpu as pltpu
from jax.sharding import PartitionSpec as P

HEAD = 64
MESH = pl.DeviceIdType.MESH
BF = jnp.bfloat16
F32 = jnp.float32
LOG2E = math.log2(math.e)

FR, FC, FD = 8, 64, 256
PR, PC = FR + 6, FC + 32
CT, CD = 128, 1024
NHEAD = 16
CHUNK = NHEAD * CT
VMEM_LIMIT = 56 * 2**20


def rms(values, gain):
    mean_square = jnp.mean(values * values, axis=-1, keepdims=True)
    return (values * lax.rsqrt(mean_square + 1e-06) * gain).astype(BF)


def head_blocks(width):
    row = lax.broadcasted_iota(jnp.int32, (width, width), 0) >> 6
    col = lax.broadcasted_iota(jnp.int32, (width, width), 1) >> 6
    return jnp.where(row == col, 1.0 / HEAD, 0.0).astype(BF)


def unit(values, blocks):
    width = blocks.shape[0]
    parts = []
    for start in range(0, values.shape[1], width):
        part = values[:, start : start + width]
        square = part * part
        high = square.astype(BF)
        low = (square - high.astype(F32)).astype(BF)
        mean = jnp.dot(high, blocks, preferred_element_type=F32) + jnp.dot(
            low, blocks, preferred_element_type=F32
        )
        parts.append(part * lax.rsqrt(mean + 1e-06))
    return parts[0] if len(parts) == 1 else jnp.concatenate(parts, axis=1)


def fine_kernel(
    image,
    gain_attn,
    w_qkv,
    scale_fine,
    w_out,
    gain_ffn,
    w_in_hbm,
    w_ffn_hbm,
    w_merge_hbm,
    gain_coarse,
    w_coarse_hbm,
    fine_out,
    coarse_in,
    kv_msg,
    q_msg,
    xpad,
    keys,
    vals,
    bias,
    attended,
    merged,
    w_in,
    w_ffn,
    w_merge,
    w_coarse,
    load_sem,
    send_sem,
    recv_sem,
):
    row, seq = lax.axis_index("rows"), lax.axis_index("seq")
    n_rows, n_seq = lax.axis_size("rows"), lax.axis_size("seq")

    loads = [
        pltpu.make_async_copy(image, xpad.at[pl.ds(3, FR), pl.ds(0, FC)], load_sem.at[0]),
        pltpu.make_async_copy(w_in_hbm, w_in, load_sem.at[1]),
        pltpu.make_async_copy(w_ffn_hbm, w_ffn, load_sem.at[2]),
        pltpu.make_async_copy(w_merge_hbm, w_merge, load_sem.at[3]),
        pltpu.make_async_copy(w_coarse_hbm, w_coarse, load_sem.at[4]),
    ]
    loads[0].start()

    barrier = pltpu.get_barrier_semaphore()
    around = [(dr, ds) for dr in (-1, 0, 1) for ds in (-1, 0, 1) if (dr, ds) != (0, 0)]
    for dr, ds in around:
        there = (lax.rem(row + dr + n_rows, n_rows), lax.rem(seq + ds + n_seq, n_seq))
        pl.semaphore_signal(barrier, inc=1, device_id=there, device_id_type=MESH)
    pl.semaphore_wait(barrier, len(around))

    source_rows = {-1: pl.ds(0, 3), 0: pl.ds(0, FR), 1: pl.ds(FR - 3, 3)}
    source_cols = {-1: pl.ds(0, 16), 0: pl.ds(0, FC), 1: pl.ds(FC - 16, 16)}
    target_rows = {-1: pl.ds(FR + 3, 3), 0: pl.ds(3, FR), 1: pl.ds(0, 3)}
    target_cols = {-1: pl.ds(FC + 16, 16), 0: pl.ds(0, FC), 1: pl.ds(FC, 16)}
    sends = []
    for i, (dr, ds) in enumerate(around):
        there = (lax.rem(row + dr + n_rows, n_rows), lax.rem(seq + ds + n_seq, n_seq))
        copy = pltpu.make_async_remote_copy(
            src_ref=image.at[source_rows[dr], source_cols[ds]],
            dst_ref=xpad.at[target_rows[dr], target_cols[ds]],
            send_sem=send_sem.at[i],
            recv_sem=recv_sem.at[i],
            device_id=there,
            device_id_type=MESH,
        )
        copy.start()
        sends.append(copy)
    for load in loads[1:]:
        load.start()

    query_col = lax.broadcasted_iota(jnp.int32, (FC, PC), 0)
    slot = lax.broadcasted_iota(jnp.int32, (FC, PC), 1)
    key_col = jnp.where(slot < FC, slot, jnp.where(slot < FC + 16, slot - FC - 16, slot - 16))
    gap = key_col - query_col
    near = jnp.where((gap >= -3) & (gap <= 3), 0.0, -1e30).astype(F32)
    bias[...] = jnp.concatenate([jnp.concatenate([near] * 7, axis=1)] * 4, axis=0)
    blocks = head_blocks(FD)
    gain = gain_attn[...]

    loads[0].wait()
    for copy in sends:
        copy.wait()

    pair = 2 * PC
    slot_col = lax.broadcasted_iota(jnp.int32, (pair, 1), 0)
    local_row = (slot_col >= PC).astype(jnp.int32)
    slot_col = slot_col - local_row * PC
    left_out = (slot_col >= FC) & (slot_col < FC + 16) & (seq == 0)
    right_out = (slot_col >= FC + 16) & (seq == n_seq - 1)

    def project(i, carry):
        normed = rms(xpad[pl.ds(i * 2, 2)].reshape(pair, FD).astype(F32), gain)
        kv = jnp.dot(normed, w_qkv[:, FD:], preferred_element_type=F32).astype(BF)
        start = pl.multiple_of(i * pair, pair)
        keys[pl.ds(start, pair), :] = unit(kv[:, :FD].astype(F32), blocks).astype(BF)
        global_row = row * FR + i * 2 + local_row - 3
        valid = (global_row >= 0) & (global_row < n_rows * FR)
        inside = jnp.where(valid & jnp.logical_not(left_out) & jnp.logical_not(right_out), 1.0, 0.0)
        value = jnp.concatenate(
            [kv[:, FD:].astype(F32) * inside, jnp.broadcast_to(inside, (pair, 128))], axis=1
        )
        vals[pl.ds(start, pair), :] = value.astype(BF)
        return carry

    lax.fori_loop(0, PR // 2, project, 0)

    lane_head = lax.broadcasted_iota(jnp.int32, (FC, FD), 1) >> 6
    factor = jnp.concatenate(
        [jnp.full((FC, 1), scale_fine[0, h] * (LOG2E / HEAD), F32) for h in range(4)], axis=0
    )

    def attend(r, carry):
        normed = rms(xpad[r + 3, 0:FC].astype(F32), gain)
        query = jnp.dot(normed, w_qkv[:, :FD], preferred_element_type=F32).astype(BF)
        query = unit(query.astype(F32), blocks)
        stacked = jnp.concatenate(
            [jnp.where(lane_head == h, query, 0.0).astype(BF) for h in range(4)], axis=0
        )
        window = pl.ds(pl.multiple_of(r * PC, PC), 7 * PC)
        scores = lax.dot_general(
            stacked, keys[window, :], (((1,), (1,)), ((), ())), preferred_element_type=F32
        )
        weights = jnp.exp2(scores * factor + bias[...]).astype(BF)
        total = jnp.dot(weights, vals[window, :], preferred_element_type=F32)
        inverse = 1.0 / total[:, FD:]
        scaled = total[:, :FD] * jnp.concatenate([inverse, inverse], axis=1)
        picked = jnp.where(lane_head == 0, scaled[:FC], 0.0)
        for h in range(1, 4):
            picked = jnp.where(lane_head == h, scaled[h * FC : (h + 1) * FC], picked)
        attended[pl.ds(pl.multiple_of(r * FC, FC), FC), :] = picked.astype(BF)
        return carry

    lax.fori_loop(0, FR, attend, 0)

    loads[1].wait()
    loads[2].wait()
    hidden = w_ffn.shape[0]
    take = lax.broadcasted_iota(jnp.int32, (128, 128), 0)
    come = lax.broadcasted_iota(jnp.int32, (128, 128), 1)
    wanted = (take >> 6) * 64 + (take & 31) * 2 + ((take >> 5) & 1)
    permute = jnp.where(come == wanted, 1.0, 0.0).astype(BF)
    gain_f = gain_ffn[...]

    def feed(i, carry):
        tokens = pl.ds(pl.multiple_of(i * 128, 128), 128)
        x = xpad[pl.ds(i * 2 + 3, 2), 0:FC].reshape(128, FD).astype(F32)
        stream = x + jnp.dot(attended[tokens, :], w_out[...], preferred_element_type=F32)
        mixed = jnp.dot(rms(stream, gain_f), w_in[...], preferred_element_type=F32)
        gated = (mixed[:, :hidden] * jax.nn.gelu(mixed[:, hidden:])).astype(BF)
        fine = (stream + jnp.dot(gated, w_ffn[...], preferred_element_type=F32)).astype(BF)
        fine_out[tokens, :] = fine
        sorted_rows = jnp.dot(permute, fine, preferred_element_type=F32).astype(BF)
        merged[pl.ds(pl.multiple_of(i * 32, 32), 32), :] = jnp.concatenate(
            [sorted_rows[j * 32 : (j + 1) * 32] for j in range(4)], axis=1
        )
        return carry

    lax.fori_loop(0, FR // 2, feed, 0)

    loads[3].wait()
    coarse = jnp.dot(merged[...], w_merge[...], preferred_element_type=F32).astype(BF)
    coarse_in[...] = coarse
    normed = rms(coarse.astype(F32), gain_coarse[...])
    loads[4].wait()
    low_half = lax.broadcasted_iota(jnp.int32, (CT, 128), 1) < HEAD

    def heads(p, carry):
        def part(which):
            cols = pl.ds(pl.multiple_of(which * CD + p * 256, 256), 256)
            return (
                jnp.dot(normed, w_coarse[:, cols], preferred_element_type=F32)
                .astype(BF)
                .astype(F32)
            )

        query = unit(part(0), blocks)
        key = unit(part(1), blocks)
        value = part(2)
        for j in range(2):
            k2 = key[:, j * 128 : (j + 1) * 128]
            v2 = value[:, j * 128 : (j + 1) * 128]
            even = jnp.where(low_half, k2, pltpu.roll(v2, HEAD, 1))
            odd = jnp.where(low_half, pltpu.roll(k2, HEAD, 1), v2)
            kv_msg[p * 4 + j * 2] = even.astype(BF)
            kv_msg[p * 4 + j * 2 + 1] = odd.astype(BF)
            q2 = query[:, j * 128 : (j + 1) * 128].T.astype(BF)
            q_msg[p * 4 + j * 2] = q2[:HEAD]
            q_msg[p * 4 + j * 2 + 1] = q2[HEAD:]
        return carry

    lax.fori_loop(0, 4, heads, 0)


def coarse_kernel(
    kv_msg,
    q_msg,
    coarse_in,
    scale_coarse,
    w_out_hbm,
    out,
    kv_buf,
    q_buf,
    q_full,
    acc,
    o_buf,
    back,
    w_out,
    load_sem,
    kv_send,
    kv_recv,
    q_send,
    q_recv,
    o_send,
    o_recv,
    g_send,
    g_recv,
):
    row, seq = lax.axis_index("rows"), lax.axis_index("seq")
    x, y, z_lo = row // 8, lax.rem(row // 2, 4), lax.rem(row, 2)
    z_hi, core = seq // 2, lax.rem(seq, 2)
    z = z_hi * 2 + z_lo
    head = y * 4 + z

    def at(dy, dz):
        py, pz = lax.rem(y + dy + 4, 4), lax.rem(z + dz + 4, 4)
        return (x * 8 + py * 2 + lax.rem(pz, 2), (pz // 2) * 2 + core), py * 4 + pz

    sibling = (row, seq + 1 - 2 * core)
    up = (lax.rem(row + 8, 32), seq)
    down = (lax.rem(row + 24, 32), seq)

    load = pltpu.make_async_copy(w_out_hbm, w_out, load_sem)
    load.start()

    offsets = [(dy, dz) for dy in range(4) for dz in range(4)]
    barrier = pltpu.get_barrier_semaphore()
    for dy, dz in offsets[1:]:
        pl.semaphore_signal(barrier, inc=1, device_id=at(dy, dz)[0], device_id_type=MESH)
    for there in (sibling, up, down):
        pl.semaphore_signal(barrier, inc=1, device_id=there, device_id_type=MESH)
    pl.semaphore_wait(barrier, 18)

    def remote(src, dst, send, recv, there):
        copy = pltpu.make_async_remote_copy(
            src_ref=src,
            dst_ref=dst,
            send_sem=send,
            recv_sem=recv,
            device_id=there,
            device_id_type=MESH,
        )
        copy.start()
        return copy

    q_copies, kv_copies = [], []
    for k, (dy, dz) in enumerate(offsets):
        if k == 0:
            continue
        there, their_head = at(dy, dz)
        q_copies.append(
            remote(q_msg.at[their_head], q_buf.at[k], q_send.at[k], q_recv.at[k], there)
        )
        kv_copies.append(
            remote(
                kv_msg.at[their_head],
                kv_buf.at[0, pl.ds(k * CT, CT)],
                kv_send.at[k],
                kv_recv.at[k],
                there,
            )
        )
    kv_buf[0, 0:CT, :] = kv_msg[head]
    q_full[0:HEAD, 0:CT] = q_msg[head]
    q_full[HEAD:, :] = jnp.zeros((HEAD, CHUNK), BF)
    acc[...] = jnp.zeros_like(acc)
    for copy in kv_copies:
        copy.wait()

    half = CHUNK // 2
    first, second = pl.ds(0, half), pl.ds(half, half)
    gathers = {}

    def gather(name, src, dst, there):
        i = len(gathers)
        gathers[name] = remote(src, dst, g_send.at[i], g_recv.at[i], there)

    gather("up", kv_buf.at[0], kv_buf.at[2], up)
    gather("down", kv_buf.at[0], kv_buf.at[4], down)
    gather("own", kv_buf.at[0], kv_buf.at[1], sibling)

    for copy in q_copies:
        copy.wait()
    for k in range(1, 16):
        q_full[0:HEAD, k * CT : (k + 1) * CT] = q_buf[k]

    factor = scale_coarse[0, head] * (LOG2E / HEAD)
    ones = jnp.ones((8, 1024), BF)

    def process(slot):
        def block(i, carry):
            kv = kv_buf[slot, pl.ds(pl.multiple_of(i * 1024, 1024), 1024), :]
            lhs = jnp.concatenate([kv.T[HEAD:], ones], axis=0)
            for u in range(2):
                cols = slice(u * 1024, (u + 1) * 1024)
                scores = jnp.dot(kv, q_full[:, cols], preferred_element_type=F32)
                weights = jnp.exp2(scores * factor).astype(BF)
                acc[:, cols] += jnp.dot(lhs, weights, preferred_element_type=F32)
            return carry

        lax.fori_loop(0, CHUNK // 1024, block, 0)

    process(0)
    gathers["own"].wait_recv()
    process(1)
    gathers["up"].wait_recv()
    gather("up2", kv_buf.at[2, first], kv_buf.at[6, first], up)
    gather("up_sib", kv_buf.at[2], kv_buf.at[3], sibling)
    gathers["down"].wait_recv()
    gather("down2", kv_buf.at[4, second], kv_buf.at[6, second], down)
    gather("down_sib", kv_buf.at[4], kv_buf.at[5], sibling)
    process(2)
    process(4)
    gathers["up_sib"].wait_recv()
    process(3)
    gathers["up2"].wait_recv()
    gathers["down2"].wait_recv()
    gather("two_sib", kv_buf.at[6], kv_buf.at[7], sibling)
    gathers["down_sib"].wait_recv()
    process(5)
    process(6)
    gathers["two_sib"].wait_recv()
    process(7)

    inverse = 1.0 / acc[HEAD : HEAD + 1, :]
    attended = (acc[0:HEAD, :] * inverse).astype(BF)
    o_copies = []
    for k, (dy, dz) in enumerate(offsets):
        part = attended[:, k * CT : (k + 1) * CT]
        if k == 0:
            back[head] = part
            continue
        o_buf[k] = part
        there = at(-dy, -dz)[0]
        o_copies.append(remote(o_buf.at[k], back.at[head], o_send.at[k], o_recv.at[k], there))
    for copy in gathers.values():
        copy.wait_send()
    load.wait()
    for copy in o_copies:
        copy.wait()
    features = back[...].reshape(CD, CT)
    product = lax.dot_general(
        features, w_out[...], (((0,), (0,)), ((), ())), preferred_element_type=F32
    )
    out[...] = (coarse_in[...].astype(F32) + product).astype(BF)


def body(
    image,
    gain_attn,
    w_qkv_fine,
    scale_fine,
    w_out_fine,
    gain_ffn,
    w_ffn_in,
    w_ffn_out,
    w_merge,
    gain_coarse,
    w_qkv_coarse,
    scale_coarse,
    w_out_coarse,
):
    vmem = pl.BlockSpec(memory_space=pltpu.VMEM)
    smem = pl.BlockSpec(memory_space=pltpu.SMEM)
    hbm = pl.BlockSpec(memory_space=pl.ANY)
    dma = pltpu.SemaphoreType.DMA
    fine_out, coarse_in, kv_msg, q_msg = pl.pallas_call(
        fine_kernel,
        out_shape=(
            jax.ShapeDtypeStruct((FR * FC, FD), BF),
            jax.ShapeDtypeStruct((CT, CD), BF),
            jax.ShapeDtypeStruct((NHEAD, CT, 128), BF),
            jax.ShapeDtypeStruct((NHEAD, HEAD, CT), BF),
        ),
        in_specs=[hbm, vmem, vmem, smem, vmem, vmem, hbm, hbm, hbm, vmem, hbm],
        out_specs=(vmem, vmem, vmem, vmem),
        scratch_shapes=[
            pltpu.VMEM((PR, PC, FD), BF),
            pltpu.VMEM((PR * PC, FD), BF),
            pltpu.VMEM((PR * PC, FD + 128), BF),
            pltpu.VMEM((4 * FC, 7 * PC), F32),
            pltpu.VMEM((FR * FC, FD), BF),
            pltpu.VMEM((CT, CD), BF),
            pltpu.VMEM(w_ffn_in.shape, BF),
            pltpu.VMEM(w_ffn_out.shape, BF),
            pltpu.VMEM(w_merge.shape, BF),
            pltpu.VMEM(w_qkv_coarse.shape, BF),
            dma((5,)),
            dma((8,)),
            dma((8,)),
        ],
        compiler_params=pltpu.CompilerParams(
            collective_id=0, has_side_effects=True, vmem_limit_bytes=VMEM_LIMIT
        ),
        name="fine",
    )(
        image,
        gain_attn.reshape(1, -1),
        w_qkv_fine,
        scale_fine.reshape(1, -1),
        w_out_fine,
        gain_ffn.reshape(1, -1),
        w_ffn_in,
        w_ffn_out,
        w_merge,
        gain_coarse.reshape(1, -1),
        w_qkv_coarse,
    )
    coarse_out = pl.pallas_call(
        coarse_kernel,
        out_shape=jax.ShapeDtypeStruct((CT, CD), BF),
        in_specs=[vmem, vmem, vmem, smem, hbm],
        out_specs=vmem,
        scratch_shapes=[
            pltpu.VMEM((8, CHUNK, 128), BF),
            pltpu.VMEM((NHEAD, HEAD, CT), BF),
            pltpu.VMEM((128, CHUNK), BF),
            pltpu.VMEM((HEAD + 8, CHUNK), F32),
            pltpu.VMEM((NHEAD, HEAD, CT), BF),
            pltpu.VMEM((NHEAD, HEAD, CT), BF),
            pltpu.VMEM(w_out_coarse.shape, BF),
            dma,
            dma((16,)),
            dma((16,)),
            dma((16,)),
            dma((16,)),
            dma((16,)),
            dma((16,)),
            dma((8,)),
            dma((8,)),
        ],
        compiler_params=pltpu.CompilerParams(
            collective_id=1, has_side_effects=True, vmem_limit_bytes=VMEM_LIMIT
        ),
        name="coarse",
    )(kv_msg, q_msg, coarse_in, scale_coarse.reshape(1, -1), w_out_coarse)
    return fine_out.reshape(image.shape), coarse_out.reshape(FR // 2, FC // 2, CD)


def solution(mesh):
    placed = (P("rows", "seq", None),) + (P(),) * 12
    return jax.shard_map(
        body,
        mesh=mesh,
        in_specs=placed,
        out_specs=(P("rows", "seq", None), P("rows", "seq", None)),
        check_vma=False,
    )
```

time: 824 us -> 101 us (0.12)
  waiting for transfers between devices: 335 us -> 0 us
  local copies, waits for them, and re-layouts: 266 us -> 2.38 us
  matrix products: 134 us -> 0 us
  Pallas kernels: 0 us -> 96.4 us
  blocking collectives: 26.2 us -> 0 us
  other arithmetic: 25.3 us -> 0 us
  starting transfers between devices: 14.6 us -> 0 us
  between operations: 14.9 us -> 0.67 us
    all_gather x2 -> x0, waiting for transfers between devices: 330 us -> none  [the longest x1 188 us: body(): lax.all_gather(moved[:, 2, 0], 'rows', axis=0, tiled=True)]
    dot_general x73 -> x0, matrix products: 134 us -> none  [the longest x32 62.1 us: block_step(): jnp.einsum('qhe,khe->hqk', queries, key_block, preferred_element_type=jnp...]
    slice x28 -> x0, local copies, waits for them, and re-layouts: 121 us -> none  [the longest x22 113 us: window_tiles(): bands[:, :, start_col:start_col + col_count:16]]
    pallas_call x0 -> x2, Pallas kernels: none -> 96.4 us  [the longest x1 61.4 us: body(): pl.pallas_call(coarse_kernel, out_shape=jax.ShapeDtypeStruct((CT, CD), BF...]
    unnamed x64 -> x4, local copies, waits for them, and re-layouts: 68.4 us -> 2.38 us
    reshape x8 -> x0, local copies, waits for them, and re-layouts: 59.3 us -> none  [the longest x1 24.5 us: fold_keys(): value_part.reshape(key_count // block_size, block_size, group_heads, HEAD)]
    all_to_all x2 -> x0, blocking collectives: 26.2 us -> none  [the longest x1 13.7 us: body(): lax.all_to_all(stacked, 'seq', split_axis=2, concat_axis=0, tiled=True)]
    ppermute x4 -> x0, starting transfers between devices: 14.5 us -> none  [the longest x2 11.1 us: extended(): before = lax.ppermute(last, axis, up)]
  transfers between devices with their start and end apart: 6 -> 0, of which waited for: 3 -> 0; matrix products, arithmetic and copies ran while one was open for 7% -> 0% of each run, Pallas kernels for 0% -> 0%
where the time goes in v1:
time: 101 us; the launch traced here: 99.5 us
  Pallas kernels  96.4 us (95%)
  local copies, waits for them, and re-layouts  2.38 us (2%)
    pallas_call x1, Pallas kernels, body(): pl.pallas_call(coarse_kernel, out_shape=jax.ShapeDtypeStruct((CT, CD), BF...  61.4 us
    pallas_call x1, Pallas kernels, body(): pl.pallas_call(fine_kernel, out_shape=(jax.ShapeDtypeStruct((FR * FC, FD)...  35 us
    unnamed x4, local copies, waits for them, and re-layouts  2.38 us

profile of v1, /device:TPU:1, one launch (start us, length us, event | category | flops | bytes accessed | tf_op | source)
XLA Modules:
  0.0 99.5 jit_solution(14106261421475706965)
XLA Ops:
  0.6 35.0 %fine.1 = (bf16[512,256]{1,0:T(8,128)(2,1)}, bf16[128,1024]{1,0:T(8,128)(2,1)}, bf16[16,128,128]{2,1,0:T(8,128)(2,1)}, bf16[16,64,128]{2,1,0:T(8,128)(2,1)}) custom-call(bf16[8,64,256]{2,1,0:T(8,128)(2,1)} %image.1, f32[1,256]{1,0:T(1,128)} %bitcast.10, bf16[256,768]{1,0:T(8,128)(2,1)} %w_qkv.1, f32[1,4]{1,0:T(1,128)} %bitcast.12, bf16[256,256]{1,0:T(8,128)(2,1)} %w_out.1, ...), custom_call_target="tpu_custom_call" | custom-call | tf_op jit(solution)/shard_map/fine/pallas_call | solution.py:425
  35.7 0.0 copy-start
  35.7 61.4 %coarse.1 = bf16[128,1024]{1,0:T(8,128)(2,1)} custom-call(bf16[16,128,128]{2,1,0:T(8,128)(2,1)} %get-tuple-element.7.kv_msg, bf16[16,64,128]{2,1,0:T(8,128)(2,1)} %get-tuple-element.8.q_msg, bf16[128,1024]{1,0:T(8,128)(2,1)} %get-tuple-element.9.coarse_in, f32[1,16]{1,0:T(1,128)} %bitcast.13, bf16[1024,1024]{1,0:T(8,128)(2,1)} %w_out_hbm.1), custom_call_target="tpu_custom_call" | custom-call | tf_op jit(solution)/shard_map/coarse/pallas_call | solution.py:467
  97.1 0.0 copy-done
  97.1 0.7 copy.17
  97.8 1.7 %copy.18 = bf16[4,32,1024]{2,1,0:T(8,128)(2,1)} copy(bf16[4,32,1024]{2,1,0:T(8,128)(2,1)} %bitcast.7) | data formatting | bytes 524288
Async XLA Ops:
  35.7 61.4 %copy-start = (bf16[512,256]{1,0:T(8,128)(2,1)S(1)}, bf16[512,256]{1,0:T(8,128)(2,1)}, u32[]{:S(2)}) copy-start(bf16[512,256]{1,0:T(8,128)(2,1)} %get-tuple-element.6) | copy-start | bytes 786436

commit v2 on v0

v2 whole, which is shorter than its diff:
```python
import math

import jax
import jax.numpy as jnp
from jax import lax
from jax.experimental import pallas as pl
from jax.experimental.pallas import tpu as pltpu
from jax.sharding import PartitionSpec as P

HEAD = 64
MESH = pl.DeviceIdType.MESH
BF = jnp.bfloat16
F32 = jnp.float32
LOG2E = math.log2(math.e)

FR, FC, FD = 8, 64, 256
PR, PC = FR + 6, FC + 32
CT, CD = 128, 1024
NHEAD = 16
QUERIES = NHEAD * CT
BLOCK = 1024
NBLOCK = 16
ORDER = (1, 2, 3, 0)
VMEM_LIMIT = 56 * 2**20


def rms(values, gain):
    mean_square = jnp.mean(values * values, axis=-1, keepdims=True)
    return (values * lax.rsqrt(mean_square + 1e-06) * gain).astype(BF)


def dot(a, b):
    return jnp.dot(a, b, preferred_element_type=F32)


def unit(values, blocks):
    square = values * values
    high = square.astype(BF)
    low = (square - high.astype(F32)).astype(BF)
    return values * lax.rsqrt(dot(high, blocks) + dot(low, blocks) + 1e-06)


def kernel(
    image,
    gain_attn,
    w_qkv_hbm,
    scale_fine,
    w_proj_hbm,
    gain_ffn,
    w_in_hbm,
    w_ffn_hbm,
    w_merge_hbm,
    gain_coarse,
    w_coarse_hbm,
    scale_coarse,
    w_out_hbm,
    fine_out,
    out,
    xpad,
    queries,
    keys,
    vals,
    bias,
    attended,
    merged,
    coarse_in,
    kv_msg,
    q_msg,
    kv_buf,
    q_buf,
    q_full,
    acc,
    o_buf,
    back,
    w_qkv,
    w_proj,
    w_in,
    w_ffn,
    w_merge,
    w_coarse,
    w_out,
    load_sem,
    halo_send,
    halo_recv,
    q_send,
    q_recv,
    kv_send,
    kv_recv,
    g_send,
    g_recv,
    o_send,
    o_recv,
):
    row, seq = lax.axis_index("rows"), lax.axis_index("seq")
    n_rows, n_seq = lax.axis_size("rows"), lax.axis_size("seq")
    x, y, z_lo = row // 8, lax.rem(row // 2, 4), lax.rem(row, 2)
    z_hi, core = seq // 2, lax.rem(seq, 2)
    z = z_hi * 2 + z_lo
    head = y * 4 + z

    def at(dy, dz):
        py, pz = lax.rem(y + dy + 4, 4), lax.rem(z + dz + 4, 4)
        return (x * 8 + py * 2 + lax.rem(pz, 2), (pz // 2) * 2 + core)

    def beside(dr, ds):
        return (lax.rem(row + dr + n_rows, n_rows), lax.rem(seq + ds + n_seq, n_seq))

    sibling = (row, seq + 1 - 2 * core)
    up = (lax.rem(row + 8, 32), seq)
    down = (lax.rem(row + 24, 32), seq)
    around = [(dr, ds) for dr in (0, -1, 1) for ds in (0, -1, 1) if (dr, ds) != (0, 0)]
    partners = [(dy, dz) for dy in ORDER for dz in range(4)]
    own = partners.index((0, 0))

    barrier = pltpu.get_barrier_semaphore()
    everyone = [beside(dr, ds) for dr, ds in around]
    everyone += [at(dy, dz) for k, (dy, dz) in enumerate(partners) if k != own]
    everyone += [sibling, up, down]
    for there in everyone:
        pl.semaphore_signal(barrier, inc=1, device_id=there, device_id_type=MESH)

    def load(source, target, i):
        copy = pltpu.make_async_copy(source, target, load_sem.at[i])
        copy.start()
        return copy

    image_load = load(image, xpad.at[pl.ds(3, FR), pl.ds(0, FC)], 0)
    w_qkv_load = load(w_qkv_hbm, w_qkv, 1)
    w_proj_load = load(w_proj_hbm, w_proj, 2)
    w_in_load = load(w_in_hbm, w_in, 3)
    w_ffn_load = load(w_ffn_hbm, w_ffn, 4)
    w_merge_load = load(w_merge_hbm, w_merge, 5)
    w_coarse_load = load(w_coarse_hbm, w_coarse, 6)
    w_out_load = load(w_out_hbm, w_out, 7)

    def remote(src, dst, send, recv, there):
        return pltpu.make_async_remote_copy(
            src_ref=src,
            dst_ref=dst,
            send_sem=send,
            recv_sem=recv,
            device_id=there,
            device_id_type=MESH,
        )

    image_load.wait()
    pl.semaphore_wait(barrier, len(everyone))

    source_rows = {-1: pl.ds(3, 3), 0: pl.ds(3, FR), 1: pl.ds(FR, 3)}
    source_cols = {-1: pl.ds(0, 16), 0: pl.ds(0, FC), 1: pl.ds(FC - 16, 16)}
    target_rows = {-1: pl.ds(FR + 3, 3), 0: pl.ds(3, FR), 1: pl.ds(0, 3)}
    target_cols = {-1: pl.ds(FC + 16, 16), 0: pl.ds(0, FC), 1: pl.ds(FC, 16)}
    halo = [
        remote(
            xpad.at[source_rows[dr], source_cols[ds]],
            xpad.at[target_rows[dr], target_cols[ds]],
            halo_send.at[i],
            halo_recv.at[i],
            beside(dr, ds),
        )
        for i, (dr, ds) in enumerate(around)
    ]
    for copy in halo:
        copy.start()

    group = (lax.broadcasted_iota(jnp.int32, (FD, FD), 0) >> 6) == (
        lax.broadcasted_iota(jnp.int32, (FD, FD), 1) >> 6
    )
    blocks = jnp.where(group, 1.0 / HEAD, 0.0).astype(BF)
    gain = gain_attn[...]
    w_qkv_load.wait()

    def project(tokens, first):
        normed = rms(tokens.astype(F32), gain)
        return dot(normed, w_qkv[:, first:]).astype(BF)

    for i in range(2):
        rows_here = slice(3 + 4 * i, 7 + 4 * i)
        triple = project(xpad[rows_here, 0:FC].reshape(4 * FC, FD), 0)
        queries[i * 4 * FC : (i + 1) * 4 * FC, :] = unit(triple[:, :FD].astype(F32), blocks).astype(
            BF
        )
        unit_keys = unit(triple[:, FD : 2 * FD].astype(F32), blocks).astype(BF)
        keys[rows_here, 0:FC] = unit_keys.reshape(4, FC, FD)
        vals[rows_here, 0:FC] = triple[:, 2 * FD :].reshape(4, FC, FD)

    query_col = lax.broadcasted_iota(jnp.int32, (FC, PC), 0)
    slot = lax.broadcasted_iota(jnp.int32, (FC, PC), 1)
    key_col = jnp.where(slot < FC, slot, jnp.where(slot < FC + 16, slot - FC - 16, slot - 16))
    gap = key_col - query_col
    near = jnp.where((gap >= -3) & (gap <= 3), 0.0, -1e30).astype(F32)
    never = jnp.full((FC, PC), -1e30, F32)
    for r in range(2):
        one = jnp.concatenate([near if r <= j <= r + 6 else never for j in range(8)], axis=1)
        for h in range(4):
            start = (r * 4 + h) * FC
            bias[start : start + FC, :] = one

    for copy in halo:
        copy.wait()

    def halo_keys(pair):
        kv = pair
        return unit(kv[:, :FD].astype(F32), blocks).astype(BF), kv[:, FD:]

    side_keys, side_vals = halo_keys(project(xpad[:, FC:].reshape(PR * 32, FD), FD))
    keys[:, FC:] = side_keys.reshape(PR, 32, FD)
    vals[:, FC:] = side_vals.reshape(PR, 32, FD)
    for rows_here in (slice(0, 3), slice(FR + 3, FR + 6)):
        end_keys, end_vals = halo_keys(project(xpad[rows_here, 0:FC].reshape(3 * FC, FD), FD))
        keys[rows_here, 0:FC] = end_keys.reshape(3, FC, FD)
        vals[rows_here, 0:FC] = end_vals.reshape(3, FC, FD)

    lane_head = lax.broadcasted_iota(jnp.int32, (FC, FD), 1) >> 6
    factor = jnp.concatenate(
        [jnp.full((FC, 1), scale_fine[0, h] * (LOG2E / HEAD), F32) for h in range(4)] * 2, axis=0
    )
    lane = lax.broadcasted_iota(jnp.int32, (1, 8 * PC), 1)
    lane_row = (lane * 683) >> 16
    lane_slot = lane - lane_row * PC
    left_out = (lane_slot >= FC) & (lane_slot < FC + 16) & (seq == 0)
    right_out = (lane_slot >= FC + 16) & (seq == n_seq - 1)
    col_bias = jnp.where(left_out | right_out, -1e30, 0.0).astype(F32)

    def attend(i, carry):
        query = queries[pl.ds(pl.multiple_of(i * 128, 128), 128), :].astype(F32)
        stacked = jnp.concatenate(
            [
                jnp.where(lane_head == h, query[r * FC : (r + 1) * FC], 0.0).astype(BF)
                for r in range(2)
                for h in range(4)
            ],
            axis=0,
        )
        window = pl.ds(i * 2, 8)
        scores = lax.dot_general(
            stacked,
            keys[window].reshape(8 * PC, FD),
            (((1,), (1,)), ((), ())),
            preferred_element_type=F32,
        )
        global_row = row * FR + i * 2 + lane_row - 3
        outside = (global_row < 0) | (global_row >= n_rows * FR)
        key_bias = jnp.where(outside, -1e30, col_bias)
        weights = jnp.exp2(scores * factor + (bias[...] + key_bias))
        total = dot(weights.astype(BF), vals[window].reshape(8 * PC, FD))
        scaled = total * (1.0 / jnp.sum(weights, axis=-1, keepdims=True))
        picked = []
        for r in range(2):
            parts = [scaled[(r * 4 + h) * FC : (r * 4 + h + 1) * FC] for h in range(4)]
            merged_heads = parts[0]
            for h in range(1, 4):
                merged_heads = jnp.where(lane_head == h, parts[h], merged_heads)
            picked.append(merged_heads)
        attended[pl.ds(pl.multiple_of(i * 128, 128), 128), :] = jnp.concatenate(
            picked, axis=0
        ).astype(BF)
        return carry

    lax.fori_loop(0, FR // 2, attend, 0)

    w_proj_load.wait()
    w_in_load.wait()
    w_ffn_load.wait()
    hidden = w_ffn.shape[0]
    take = lax.broadcasted_iota(jnp.int32, (128, 128), 0)
    come = lax.broadcasted_iota(jnp.int32, (128, 128), 1)
    wanted = (take >> 6) * 64 + (take & 31) * 2 + ((take >> 5) & 1)
    permute = jnp.where(come == wanted, 1.0, 0.0).astype(BF)
    gain_f = gain_ffn[...]
    for i in range(2):
        tokens = slice(i * 256, (i + 1) * 256)
        here = xpad[3 + 4 * i : 7 + 4 * i, 0:FC].reshape(256, FD).astype(F32)
        stream = here + dot(attended[tokens, :], w_proj[...])
        normed = rms(stream, gain_f)
        for c in range(0, hidden, 256):
            value = dot(normed, w_in[:, c : c + 256])
            gate = dot(normed, w_in[:, hidden + c : hidden + c + 256])
            gated = (value * jax.nn.gelu(gate)).astype(BF)
            stream = stream + dot(gated, w_ffn[c : c + 256, :])
        fine = stream.astype(BF)
        fine_out[tokens, :] = fine
        for j in range(2):
            part = dot(permute, fine[j * 128 : (j + 1) * 128]).astype(BF)
            start = (i * 2 + j) * 32
            merged[start : start + 32, :] = jnp.concatenate(
                [part[n * 32 : (n + 1) * 32] for n in range(4)], axis=1
            )

    w_merge_load.wait()
    coarse = dot(merged[...], w_merge[...]).astype(BF)
    coarse_in[...] = coarse
    normed = rms(coarse.astype(F32), gain_coarse[...])

    w_coarse_load.wait()

    def heads(which, dy):
        start = which * CD + lax.rem(y + dy, 4) * 256
        cols = pl.ds(pl.multiple_of(start, 256), 256)
        return dot(normed, w_coarse[:, cols]).astype(BF).astype(F32)

    low_half = lax.broadcasted_iota(jnp.int32, (CT, 128), 1) < HEAD
    q_copies, kv_copies = {}, {}
    for n, dy in enumerate(ORDER):
        query = unit(heads(0, dy), blocks)
        for j in range(2):
            turned = query[:, j * 128 : (j + 1) * 128].T.astype(BF)
            q_msg[n * 4 + 2 * j] = turned[:HEAD]
            q_msg[n * 4 + 2 * j + 1] = turned[HEAD:]
        for dz in range(4):
            k = n * 4 + dz
            if k != own:
                source = q_msg.at[n * 4 + lax.rem(z + dz, 4)]
                q_copies[k] = remote(
                    source, q_buf.at[k], q_send.at[k], q_recv.at[k], at(dy, dz)
                )
                q_copies[k].start()
    for n, dy in enumerate(ORDER):
        key = unit(heads(1, dy), blocks)
        value = heads(2, dy)
        for j in range(2):
            k2 = key[:, j * 128 : (j + 1) * 128]
            v2 = value[:, j * 128 : (j + 1) * 128]
            even = jnp.where(low_half, k2, pltpu.roll(v2, HEAD, 1))
            odd = jnp.where(low_half, pltpu.roll(k2, HEAD, 1), v2)
            kv_msg[n * 4 + 2 * j] = even.astype(BF)
            kv_msg[n * 4 + 2 * j + 1] = odd.astype(BF)
        for dz in range(4):
            k = n * 4 + dz
            if k != own:
                source = kv_msg.at[n * 4 + lax.rem(z + dz, 4)]
                target = kv_buf.at[k // 8, pl.ds((k % 8) * CT, CT)]
                kv_copies[k] = remote(source, target, kv_send.at[k], kv_recv.at[k], at(dy, dz))
                kv_copies[k].start()
    own_row = (own % 8) * CT
    kv_buf[own // 8, own_row : own_row + CT, :] = kv_msg[own + z]

    q_full[HEAD:, :] = jnp.zeros((HEAD, QUERIES), BF)
    acc[...] = jnp.zeros_like(acc)
    for k in range(16):
        if k == own:
            part = q_msg[own + z]
        else:
            q_copies[k].wait()
            part = q_buf[k]
        q_full[0:HEAD, k * CT : (k + 1) * CT] = part

    def gather(source, target, there):
        return remote(
            kv_buf.at[source], kv_buf.at[target], g_send.at[target], g_recv.at[target], there
        )

    gathers = {
        2: gather(0, 2, sibling),
        3: gather(1, 3, sibling),
        4: gather(0, 4, up),
        5: gather(0, 5, down),
        6: gather(4, 6, sibling),
        7: gather(5, 7, sibling),
        8: gather(1, 8, up),
        9: gather(1, 9, down),
        10: gather(8, 10, sibling),
        11: gather(9, 11, sibling),
        12: gather(4, 12, up),
        13: gather(9, 13, down),
        14: gather(12, 14, sibling),
        15: gather(13, 15, sibling),
    }
    arrive = {b: ("gather", (b,)) for b in gathers}
    arrive[0] = ("plane", range(0, 8))
    arrive[1] = ("plane", range(8, 16))
    arrive[8] = ("gather", (8, 9))
    arrive[12] = ("gather", (12, 13))
    del arrive[9], arrive[13]
    start_after = {0: (4, 5, 2), 1: (8, 9, 3), 4: (12, 6), 5: (7,), 8: (13, 10, 11), 12: (14, 15)}

    def arrivals(b):
        kind, which = arrive[b]
        for k in which:
            if kind == "gather":
                gathers[k].wait_recv()
            elif k != own:
                kv_copies[k].wait()
        for target in start_after.get(b, ()):
            gathers[target].start()

    head_factor = scale_coarse[0, head] * (LOG2E / HEAD)
    ones = jnp.ones((8, BLOCK), BF)
    half = QUERIES // 2

    def process(b, halves):
        kv = kv_buf[b]
        lhs = jnp.concatenate([kv.T[HEAD:], ones], axis=0)
        for u in halves:
            cols = slice(u * half, (u + 1) * half)
            weights = jnp.exp2(dot(kv, q_full[:, cols]) * head_factor).astype(BF)
            acc[:, cols] += dot(lhs, weights)

    def step(b, carry):
        for block in sorted(arrive):
            if block < 12:
                pl.when(b == block)(lambda block=block: arrivals(block))
        process(b, (0, 1))
        return carry

    lax.fori_loop(0, 12, step, 0)

    o_copies = {}
    for u in range(2):

        def last(b, carry):
            if u == 0:
                for block in (12, 14, 15):
                    pl.when(b == block)(lambda block=block: arrivals(block))
            process(b, (u,))
            return carry

        lax.fori_loop(12, NBLOCK, last, 0)
        cols = slice(u * half, (u + 1) * half)
        inverse = 1.0 / acc[HEAD : HEAD + 1, cols]
        done = (acc[0:HEAD, cols] * inverse).astype(BF)
        for k in range(u * 8, u * 8 + 8):
            dy, dz = partners[k]
            part = done[:, (k % 8) * CT : (k % 8 + 1) * CT]
            if k == own:
                back[head] = part
                continue
            o_buf[k] = part
            o_copies[k] = remote(
                o_buf.at[k], back.at[head], o_send.at[k], o_recv.at[k], at(-dy, -dz)
            )
            o_copies[k].start()

    for b in range(2, NBLOCK):
        gathers[b].wait_send()
    w_out_load.wait()
    total = coarse_in[...].astype(F32)
    for n, dy in enumerate(ORDER):
        for dz in range(4):
            if n * 4 + dz != own:
                o_copies[n * 4 + dz].wait()
        from_y = lax.rem(y + dy, 4)
        features = back[pl.ds(from_y * 4, 4)].reshape(256, CT)
        rows_here = pl.ds(pl.multiple_of(from_y * 256, 256), 256)
        total = total + lax.dot_general(
            features, w_out[rows_here, :], (((0,), (0,)), ((), ())), preferred_element_type=F32
        )
    out[...] = total.astype(BF)


def body(
    image,
    gain_attn,
    w_qkv_fine,
    scale_fine,
    w_out_fine,
    gain_ffn,
    w_ffn_in,
    w_ffn_out,
    w_merge,
    gain_coarse,
    w_qkv_coarse,
    scale_coarse,
    w_out_coarse,
):
    vmem = pl.BlockSpec(memory_space=pltpu.VMEM)
    smem = pl.BlockSpec(memory_space=pltpu.SMEM)
    hbm = pl.BlockSpec(memory_space=pl.ANY)
    dma = pltpu.SemaphoreType.DMA
    weights = (w_qkv_fine, w_out_fine, w_ffn_in, w_ffn_out, w_merge, w_qkv_coarse, w_out_coarse)
    fine_out, coarse_out = pl.pallas_call(
        kernel,
        out_shape=(pltpu.VMEM((FR * FC, FD), BF), pltpu.VMEM((CT, CD), BF)),
        in_specs=[hbm, vmem, hbm, smem, hbm, vmem, hbm, hbm, hbm, vmem, hbm, smem, hbm],
        out_specs=(vmem, vmem),
        scratch_shapes=[
            pltpu.VMEM((PR, PC, FD), BF),
            pltpu.VMEM((FR * FC, FD), BF),
            pltpu.VMEM((PR, PC, FD), BF),
            pltpu.VMEM((PR, PC, FD), BF),
            pltpu.VMEM((8 * FC, 8 * PC), F32),
            pltpu.VMEM((FR * FC, FD), BF),
            pltpu.VMEM((CT, CD), BF),
            pltpu.VMEM((CT, CD), BF),
            pltpu.VMEM((NHEAD, CT, 128), BF),
            pltpu.VMEM((NHEAD, HEAD, CT), BF),
            pltpu.VMEM((NBLOCK, BLOCK, 128), BF),
            pltpu.VMEM((NHEAD, HEAD, CT), BF),
            pltpu.VMEM((128, QUERIES), BF),
            pltpu.VMEM((HEAD + 8, QUERIES), F32),
            pltpu.VMEM((NHEAD, HEAD, CT), BF),
            pltpu.VMEM((NHEAD, HEAD, CT), BF),
        ]
        + [pltpu.VMEM(w.shape, BF) for w in weights]
        + [dma((8,)), dma((8,)), dma((8,))]
        + [dma((16,))] * 8,
        compiler_params=pltpu.CompilerParams(
            collective_id=0, has_side_effects=True, vmem_limit_bytes=VMEM_LIMIT
        ),
        name="window",
    )(
        image,
        gain_attn.reshape(1, -1),
        w_qkv_fine,
        scale_fine.reshape(1, -1),
        w_out_fine,
        gain_ffn.reshape(1, -1),
        w_ffn_in,
        w_ffn_out,
        w_merge,
        gain_coarse.reshape(1, -1),
        w_qkv_coarse,
        scale_coarse.reshape(1, -1),
        w_out_coarse,
    )
    return fine_out.reshape(image.shape), coarse_out.reshape(FR // 2, FC // 2, CD)


def solution(mesh):
    placed = (P("rows", "seq", None),) + (P(),) * 12
    return jax.shard_map(
        body,
        mesh=mesh,
        in_specs=placed,
        out_specs=(P("rows", "seq", None), P("rows", "seq", None)),
        check_vma=False,
    )
```

time: 824 us -> 78.2 us (0.09)
  waiting for transfers between devices: 335 us -> 0 us
  local copies, waits for them, and re-layouts: 266 us -> 1.41 us
  matrix products: 134 us -> 0 us
  Pallas kernels: 0 us -> 75.3 us
  blocking collectives: 26.2 us -> 0 us
  other arithmetic: 25.3 us -> 0 us
  starting transfers between devices: 14.6 us -> 0 us
  between operations: 14.9 us -> 0.64 us
    all_gather x2 -> x0, waiting for transfers between devices: 330 us -> none  [the longest x1 188 us: body(): lax.all_gather(moved[:, 2, 0], 'rows', axis=0, tiled=True)]
    dot_general x73 -> x0, matrix products: 134 us -> none  [the longest x32 62.1 us: block_step(): jnp.einsum('qhe,khe->hqk', queries, key_block, preferred_element_type=jnp...]
    slice x28 -> x0, local copies, waits for them, and re-layouts: 121 us -> none  [the longest x22 113 us: window_tiles(): bands[:, :, start_col:start_col + col_count:16]]
    pallas_call x0 -> x1, Pallas kernels: none -> 75.3 us  [body(): pl.pallas_call(kernel, out_shape=(pltpu.VMEM((FR * FC, FD), BF), pltpu.VM...]
    unnamed x64 -> x2, local copies, waits for them, and re-layouts: 68.4 us -> 1.41 us
    reshape x8 -> x0, local copies, waits for them, and re-layouts: 59.3 us -> none  [the longest x1 24.5 us: fold_keys(): value_part.reshape(key_count // block_size, block_size, group_heads, HEAD)]
    all_to_all x2 -> x0, blocking collectives: 26.2 us -> none  [the longest x1 13.7 us: body(): lax.all_to_all(stacked, 'seq', split_axis=2, concat_axis=0, tiled=True)]
    ppermute x4 -> x0, starting transfers between devices: 14.5 us -> none  [the longest x2 11.1 us: extended(): before = lax.ppermute(last, axis, up)]
  transfers between devices with their start and end apart: 6 -> 0, of which waited for: 3 -> 0; matrix products, arithmetic and copies ran while one was open for 7% -> 0% of each run, Pallas kernels for 0% -> 0%
where the time goes in v2:
time: 78.2 us; the launch traced here: 77.3 us
  Pallas kernels  75.3 us (96%)
  local copies, waits for them, and re-layouts  1.41 us (2%)
    pallas_call x1, Pallas kernels, body(): pl.pallas_call(kernel, out_shape=(pltpu.VMEM((FR * FC, FD), BF), pltpu.VM...  75.3 us

profile of v2, /device:TPU:1, one launch (start us, length us, event | category | flops | bytes accessed | tf_op | source)
XLA Modules:
  0.0 77.3 jit_solution(12120183442073754758)
XLA Ops:
  0.6 75.3 %window.1 = (bf16[512,256]{1,0:T(8,128)(2,1)S(1)}, bf16[128,1024]{1,0:T(8,128)(2,1)S(1)}) custom-call(bf16[8,64,256]{2,1,0:T(8,128)(2,1)} %image.1, f32[1,256]{1,0:T(1,128)} %bitcast.10, bf16[256,768]{1,0:T(8,128)(2,1)} %w_qkv_hbm.1, f32[1,4]{1,0:T(1,128)} %bitcast.12, bf16[256,256]{1,0:T(8,128)(2,1)} %w_proj_hbm.1, f32[1,256]{1,0:T(1,128)} %bitcast.11, ...), custom_call_target="tpu_custom_call" | custom-call | tf_op jit(solution)/shard_map/window/pallas_call | solution.py:471
  75.9 0.7 copy.17
  76.6 0.7 copy.18

commit v3 on v2

v3 whole, which is shorter than its diff:
```python
import math

import jax
import jax.numpy as jnp
from jax import lax
from jax.experimental import pallas as pl
from jax.experimental.pallas import tpu as pltpu
from jax.sharding import PartitionSpec as P

HEAD = 64
MESH = pl.DeviceIdType.MESH
BF = jnp.bfloat16
F32 = jnp.float32
LOG2E = math.log2(math.e)

FR, FC, FD = 8, 64, 256
PR = FR + 6
WINDOW = 8 * FC
SIDE = 128
CT, CD = 128, 1024
NHEAD = 16
HT = CT // 2
QUERIES = NHEAD * CT
BLOCK = 1024
NBLOCK = 16
ORDER = (1, 2, 3, 0)
VMEM_LIMIT = 56 * 2**20


def rms(values, gain):
    mean_square = jnp.mean(values * values, axis=-1, keepdims=True)
    return (values * lax.rsqrt(mean_square + 1e-06) * gain).astype(BF)


def dot(a, b):
    return jnp.dot(a, b, preferred_element_type=F32)


def unit(values, blocks):
    square = values * values
    high = square.astype(BF)
    low = (square - high.astype(F32)).astype(BF)
    return values * lax.rsqrt(dot(high, blocks) + dot(low, blocks) + 1e-06)


def kernel(
    image,
    gain_attn,
    w_qkv_hbm,
    scale_fine,
    w_proj_hbm,
    gain_ffn,
    w_in_hbm,
    w_ffn_hbm,
    w_merge_hbm,
    gain_coarse,
    w_coarse_hbm,
    scale_coarse,
    w_out_hbm,
    fine_out,
    out,
    xpad,
    packed,
    side,
    queries,
    keys,
    vals,
    side_keys,
    side_vals,
    bias,
    side_gap,
    attended,
    merged,
    coarse_in,
    messages,
    landed,
    kv_buf,
    q_buf,
    q_full,
    acc,
    o_buf,
    back,
    w_qkv,
    w_proj,
    w_in,
    w_ffn,
    w_merge,
    w_coarse,
    w_out,
    load_sem,
    halo_send,
    halo_recv,
    x_send,
    x_recv,
    g_send,
    g_recv,
    o_send,
    o_recv,
):
    row, seq = lax.axis_index("rows"), lax.axis_index("seq")
    n_rows, n_seq = lax.axis_size("rows"), lax.axis_size("seq")
    x, y, z_lo = row // 8, lax.rem(row // 2, 4), lax.rem(row, 2)
    z_hi, core = seq // 2, lax.rem(seq, 2)
    z = z_hi * 2 + z_lo
    head = y * 4 + z

    def at(dy, dz):
        py, pz = lax.rem(y + dy + 4, 4), lax.rem(z + dz + 4, 4)
        return (x * 8 + py * 2 + lax.rem(pz, 2), (pz // 2) * 2 + core)

    def beside(dr, ds):
        return (lax.rem(row + dr + n_rows, n_rows), lax.rem(seq + ds + n_seq, n_seq))

    sibling = (row, seq + 1 - 2 * core)
    up = (lax.rem(row + 8, 32), seq)
    down = (lax.rem(row + 24, 32), seq)
    around = [(dr, ds) for dr in (0, -1, 1) for ds in (0, -1, 1) if (dr, ds) != (0, 0)]
    partners = [(dy, dz) for dy in ORDER for dz in range(4)]
    own = partners.index((0, 0))

    barrier = pltpu.get_barrier_semaphore()
    everyone = [beside(dr, ds) for dr, ds in around]
    everyone += [at(dy, dz) for k, (dy, dz) in enumerate(partners) if k != own]
    everyone += [sibling, up, down]
    for there in everyone:
        pl.semaphore_signal(barrier, inc=1, device_id=there, device_id_type=MESH)

    def load(source, target, i):
        copy = pltpu.make_async_copy(source, target, load_sem.at[i])
        copy.start()
        return copy

    image_load = load(image, xpad.at[pl.ds(3, FR)], 0)
    w_qkv_load = load(w_qkv_hbm, w_qkv, 1)
    w_proj_load = load(w_proj_hbm, w_proj, 2)
    w_in_load = load(w_in_hbm, w_in, 3)
    w_ffn_load = load(w_ffn_hbm, w_ffn, 4)
    w_merge_load = load(w_merge_hbm, w_merge, 5)
    w_coarse_load = load(w_coarse_hbm, w_coarse, 6)
    w_out_load = load(w_out_hbm, w_out, 7)

    def remote(src, dst, send, recv, there):
        return pltpu.make_async_remote_copy(
            src_ref=src,
            dst_ref=dst,
            send_sem=send,
            recv_sem=recv,
            device_id=there,
            device_id_type=MESH,
        )

    image_load.wait()
    pl.semaphore_wait(barrier, len(everyone))

    halo = {}

    def send_halo(place, source, target):
        i = len(halo)
        halo[place] = remote(source, target, halo_send.at[i], halo_recv.at[i], beside(*place))
        halo[place].start()

    send_halo((-1, 0), xpad.at[pl.ds(3, 3)], xpad.at[pl.ds(FR + 3, 3)])
    send_halo((1, 0), xpad.at[pl.ds(FR, 3)], xpad.at[pl.ds(0, 3)])
    take = lax.broadcasted_iota(jnp.int32, (64, FR * FC), 0)
    come = lax.broadcasted_iota(jnp.int32, (64, FR * FC), 1)
    wanted = ((take & 31) >> 2) * FC + (take & 3) + (take >> 5) * (FC - 4)
    pick = jnp.where(come == wanted, 1.0, 0.0).astype(BF)
    packed[...] = dot(pick, xpad[3 : 3 + FR].reshape(FR * FC, FD)).astype(BF)
    for ds, start in ((-1, 0), (1, 32)):
        there = 1 if ds == -1 else 0
        send_halo((0, ds), packed.at[pl.ds(start, 32)], side.at[there, pl.ds(16, 32)])
        send_halo((-1, ds), packed.at[pl.ds(start, 16)], side.at[there, pl.ds(48, 16)])
        send_halo((1, ds), packed.at[pl.ds(start + 16, 16)], side.at[there, pl.ds(0, 16)])

    group = (lax.broadcasted_iota(jnp.int32, (FD, FD), 0) >> 6) == (
        lax.broadcasted_iota(jnp.int32, (FD, FD), 1) >> 6
    )
    blocks = jnp.where(group, 1.0 / HEAD, 0.0).astype(BF)
    gain = gain_attn[...]
    w_qkv_load.wait()

    def project(tokens, first):
        normed = rms(tokens.astype(F32), gain)
        return dot(normed, w_qkv[:, first:]).astype(BF)

    def unit_bf(values):
        return unit(values.astype(F32), blocks).astype(BF)

    for i in range(2):
        rows_here = slice(3 + 4 * i, 7 + 4 * i)
        triple = project(xpad[rows_here].reshape(4 * FC, FD), 0)
        queries[i * 4 * FC : (i + 1) * 4 * FC, :] = unit_bf(triple[:, :FD])
        keys[rows_here] = unit_bf(triple[:, FD : 2 * FD]).reshape(4, FC, FD)
        vals[rows_here] = triple[:, 2 * FD :].reshape(4, FC, FD)

    gap = lax.broadcasted_iota(jnp.int32, (FC, FC), 1) - lax.broadcasted_iota(
        jnp.int32, (FC, FC), 0
    )
    near = jnp.where((gap >= -3) & (gap <= 3), 0.0, -1e30).astype(F32)
    never = jnp.full((FC, FC), -1e30, F32)
    query_col = lax.broadcasted_iota(jnp.int32, (FC, SIDE), 0)
    slot = lax.broadcasted_iota(jnp.int32, (FC, SIDE), 1)
    right = slot >> 6
    side_row = ((slot & 63) >> 2) - 1
    side_col = (slot & 3) - 4 + right * (FC + 4)
    side_global = row * FR + side_row - 3
    side_near = (side_col - query_col >= -3) & (side_col - query_col <= 3)
    side_near = side_near & (side_global >= 0) & (side_global < n_rows * FR)
    side_near = side_near & ((right > 0) | (seq > 0)) & ((right < 1) | (seq < n_seq - 1))
    for r in range(2):
        one = jnp.concatenate([near if r <= j <= r + 6 else never for j in range(8)], axis=1)
        gap_row = jnp.where(side_near, side_row - r, 1000)
        for h in range(4):
            start = (r * 4 + h) * FC
            bias[start : start + FC, :] = one
            side_gap[start : start + FC, :] = gap_row

    lane_head = lax.broadcasted_iota(jnp.int32, (FC, FD), 1) >> 6
    factor = jnp.concatenate(
        [jnp.full((FC, 1), scale_fine[0, h] * (LOG2E / HEAD), F32) for h in range(4)] * 2, axis=0
    )
    window_row = lax.broadcasted_iota(jnp.int32, (1, WINDOW), 1) >> 6
    last_dims = (((1,), (1,)), ((), ()))

    def attend(i):
        query = queries[i * 128 : (i + 1) * 128, :].astype(F32)
        stacked = jnp.concatenate(
            [
                jnp.where(lane_head == h, query[r * FC : (r + 1) * FC], 0.0).astype(BF)
                for r in range(2)
                for h in range(4)
            ],
            axis=0,
        )
        window = slice(i * 2, i * 2 + 8)
        scores = lax.dot_general(
            stacked, keys[window].reshape(WINDOW, FD), last_dims, preferred_element_type=F32
        )
        side_scores = lax.dot_general(
            stacked, side_keys[...], last_dims, preferred_element_type=F32
        )
        global_row = row * FR + i * 2 + window_row - 3
        outside = (global_row < 0) | (global_row >= n_rows * FR)
        key_bias = jnp.where(outside, -1e30, 0.0).astype(F32)
        weights = jnp.exp2(scores * factor + (bias[...] + key_bias))
        off = side_gap[...] - i * 2
        side_weights = jnp.where(
            (off >= 0) & (off <= 6), jnp.exp2(side_scores * factor), 0.0
        )
        total = dot(weights.astype(BF), vals[window].reshape(WINDOW, FD)) + dot(
            side_weights.astype(BF), side_vals[...]
        )
        weight_sum = side_weights
        for j in range(0, WINDOW, 128):
            weight_sum = weight_sum + weights[:, j : j + 128]
        scaled = total * (1.0 / jnp.sum(weight_sum, axis=-1, keepdims=True))
        picked = []
        for r in range(2):
            parts = [scaled[(r * 4 + h) * FC : (r * 4 + h + 1) * FC] for h in range(4)]
            merged_heads = parts[0]
            for h in range(1, 4):
                merged_heads = jnp.where(lane_head == h, parts[h], merged_heads)
            picked.append(merged_heads)
        attended[i * 128 : (i + 1) * 128, :] = jnp.concatenate(picked, axis=0).astype(BF)

    def end_rows(rows_here):
        kv = project(xpad[rows_here].reshape(3 * FC, FD), FD)
        keys[rows_here] = unit_bf(kv[:, :FD]).reshape(3, FC, FD)
        vals[rows_here] = kv[:, FD:].reshape(3, FC, FD)

    hidden = w_ffn.shape[0]
    take = lax.broadcasted_iota(jnp.int32, (128, 128), 0)
    come = lax.broadcasted_iota(jnp.int32, (128, 128), 1)
    wanted = (take >> 6) * 64 + (take & 31) * 2 + ((take >> 5) & 1)
    permute = jnp.where(come == wanted, 1.0, 0.0).astype(BF)
    gain_f = gain_ffn[...]

    def feed(i):
        tokens = slice(i * 256, (i + 1) * 256)
        here = xpad[3 + 4 * i : 7 + 4 * i].reshape(256, FD).astype(F32)
        stream = here + dot(attended[tokens, :], w_proj[...])
        normed = rms(stream, gain_f)
        for c in range(0, hidden, 256):
            value = dot(normed, w_in[:, c : c + 256])
            gate = dot(normed, w_in[:, hidden + c : hidden + c + 256])
            gated = (value * jax.nn.gelu(gate)).astype(BF)
            stream = stream + dot(gated, w_ffn[c : c + 256, :])
        fine = stream.astype(BF)
        fine_out[tokens, :] = fine
        for j in range(2):
            part = dot(permute, fine[j * 128 : (j + 1) * 128]).astype(BF)
            start = (i * 2 + j) * 32
            merged[start : start + 32, :] = jnp.concatenate(
                [part[n * 32 : (n + 1) * 32] for n in range(4)], axis=1
            )

    low_half = lax.broadcasted_iota(jnp.int32, (HT, 128), 1) < HEAD
    copies = {}

    def exchange(t):
        tokens = slice(t * HT, (t + 1) * HT)
        coarse = dot(merged[tokens, :], w_merge[...]).astype(BF)
        coarse_in[tokens, :] = coarse
        normed = rms(coarse.astype(F32), gain_coarse[...])

        def heads(which, dy):
            start = which * CD + lax.rem(y + dy, 4) * 256
            cols = pl.ds(pl.multiple_of(start, 256), 256)
            return dot(normed, w_coarse[:, cols]).astype(BF).astype(F32)

        def query_part(n, dy):
            query = unit(heads(0, dy), blocks)
            for j in range(2):
                pair = query[:, j * 128 : (j + 1) * 128]
                turned = jnp.concatenate([pair, pair], axis=0).T
                for e in range(2):
                    first, second = turned[e * 64 : e * 64 + 32], turned[e * 64 + 32 : e * 64 + 64]
                    part = jnp.where(low_half[:32], first, second).astype(BF)
                    messages[t, n * 4 + 2 * j + e, HT:] = part

        def key_part(n, dy):
            key = unit(heads(1, dy), blocks)
            value = heads(2, dy)
            for j in range(2):
                k2 = key[:, j * 128 : (j + 1) * 128]
                v2 = value[:, j * 128 : (j + 1) * 128]
                even = jnp.where(low_half, k2, pltpu.roll(v2, HEAD, 1))
                odd = jnp.where(low_half, pltpu.roll(k2, HEAD, 1), v2)
                messages[t, n * 4 + 2 * j, :HT] = even.astype(BF)
                messages[t, n * 4 + 2 * j + 1, :HT] = odd.astype(BF)

        def send(n, dy, name, rows_here, target):
            for dz in range(4):
                k = n * 4 + dz
                if k != own:
                    copies[name, k] = remote(
                        messages.at[t, n * 4 + lax.rem(z + dz, 4), rows_here],
                        target(k),
                        x_send.at[name, k],
                        x_recv.at[name, k],
                        at(dy, dz),
                    )
                    copies[name, k].start()

        if t == 0:
            for n, dy in enumerate(ORDER):
                query_part(n, dy)
                key_part(n, dy)
                send(n, dy, 0, pl.ds(0, 96), lambda k: landed.at[k])
        else:
            for n, dy in enumerate(ORDER):
                query_part(n, dy)
                send(n, dy, 1, pl.ds(HT, 32), lambda k: q_buf.at[k])
            for n, dy in enumerate(ORDER):
                key_part(n, dy)
                send(n, dy, 2, pl.ds(0, HT), lambda k: kv_buf.at[2, pl.ds(k * HT, HT)])
            kv_buf[2, own * HT : (own + 1) * HT, :] = messages[1, own + z, :HT]

    for place in halo:
        if place != (1, 0) and place != (-1, 0):
            halo[place].wait()
    side_kv = project(side[...].reshape(SIDE, FD), FD)
    side_keys[...] = unit_bf(side_kv[:, :FD])
    side_vals[...] = side_kv[:, FD:]
    halo[1, 0].wait()
    end_rows(slice(0, 3))
    attend(0)
    attend(1)
    w_proj_load.wait()
    w_in_load.wait()
    w_ffn_load.wait()
    feed(0)
    w_merge_load.wait()
    w_coarse_load.wait()
    exchange(0)
    halo[-1, 0].wait()
    end_rows(slice(FR + 3, FR + 6))
    attend(2)
    attend(3)
    feed(1)
    exchange(1)

    q_full[HEAD:, :] = jnp.zeros((HEAD, QUERIES), BF)
    acc[...] = jnp.zeros_like(acc)
    def gather(source, target, there):
        return remote(
            kv_buf.at[source], kv_buf.at[target], g_send.at[target], g_recv.at[target], there
        )

    gathers = {
        1: gather(0, 1, sibling),
        3: gather(2, 3, sibling),
        4: gather(0, 4, up),
        5: gather(0, 5, down),
        6: gather(4, 6, sibling),
        7: gather(5, 7, sibling),
        8: gather(2, 8, up),
        9: gather(2, 9, down),
        10: gather(8, 10, sibling),
        11: gather(9, 11, sibling),
        12: gather(4, 12, up),
        13: gather(9, 13, down),
        14: gather(12, 14, sibling),
        15: gather(13, 15, sibling),
    }
    arrive = {b: ("gather", (b,)) for b in gathers}
    arrive[0] = ("plane", [(0, k) for k in range(16)])
    arrive[2] = ("plane", [(2, k) for k in range(16)])
    arrive[8] = ("gather", (8, 9))
    arrive[12] = ("gather", (12, 13))
    del arrive[9], arrive[13]
    start_after = {0: (4, 5, 1), 2: (8, 9, 3), 4: (12, 6), 5: (7,), 8: (13, 10, 11), 12: (14, 15)}

    def arrivals(b):
        kind, which = arrive[b]
        for k in which:
            if kind == "gather":
                gathers[k].wait_recv()
            elif k[1] != own:
                copies[k].wait()
        if b == 0:
            for k in range(16):
                part = messages[0, own + z, :HT] if k == own else landed[k, :HT]
                kv_buf[0, k * HT : (k + 1) * HT, :] = part
        for target in start_after.get(b, ()):
            gathers[target].start()

    arrivals(0)
    for k in range(16):
        if k == own:
            parts = [messages[t, own + z, HT:] for t in range(2)]
        else:
            copies[1, k].wait()
            parts = [landed[k, HT:], q_buf[k]]
        parts = [part.astype(F32) for part in parts]
        top = jnp.where(low_half[:32], parts[0], pltpu.roll(parts[1], HEAD, 1))
        end = jnp.where(low_half[:32], pltpu.roll(parts[0], HEAD, 1), parts[1])
        q_full[0:HEAD, k * CT : (k + 1) * CT] = jnp.concatenate([top, end], axis=0).astype(BF)

    head_factor = scale_coarse[0, head] * (LOG2E / HEAD)
    ones = jnp.ones((8, BLOCK), BF)
    half = QUERIES // 2

    def process(b, halves):
        kv = kv_buf[b]
        lhs = jnp.concatenate([kv.T[HEAD:], ones], axis=0)
        for u in halves:
            cols = slice(u * half, (u + 1) * half)
            weights = jnp.exp2(dot(kv, q_full[:, cols]) * head_factor).astype(BF)
            acc[:, cols] += dot(lhs, weights)

    def step(b, carry):
        for block in sorted(arrive):
            if 0 < block < 12:
                pl.when(b == block)(lambda block=block: arrivals(block))
        process(b, (0, 1))
        return carry

    lax.fori_loop(0, 12, step, 0)

    o_copies = {}
    for u in range(2):

        def last(b, carry):
            if u == 0:
                for block in (12, 14, 15):
                    pl.when(b == block)(lambda block=block: arrivals(block))
            process(b, (u,))
            return carry

        lax.fori_loop(12, NBLOCK, last, 0)
        cols = slice(u * half, (u + 1) * half)
        inverse = 1.0 / acc[HEAD : HEAD + 1, cols]
        done = (acc[0:HEAD, cols] * inverse).astype(BF)
        for k in range(u * 8, u * 8 + 8):
            dy, dz = partners[k]
            part = done[:, (k % 8) * CT : (k % 8 + 1) * CT]
            if k == own:
                back[head] = part
                continue
            o_buf[k] = part
            o_copies[k] = remote(
                o_buf.at[k], back.at[head], o_send.at[k], o_recv.at[k], at(-dy, -dz)
            )
            o_copies[k].start()

    for copy in gathers.values():
        copy.wait_send()
    w_out_load.wait()
    total = coarse_in[...].astype(F32)
    for n, dy in enumerate(ORDER):
        for dz in range(4):
            if n * 4 + dz != own:
                o_copies[n * 4 + dz].wait()
        from_y = lax.rem(y + dy, 4)
        features = back[pl.ds(from_y * 4, 4)].reshape(256, CT)
        rows_here = pl.ds(pl.multiple_of(from_y * 256, 256), 256)
        total = total + lax.dot_general(
            features, w_out[rows_here, :], (((0,), (0,)), ((), ())), preferred_element_type=F32
        )
    out[...] = total.astype(BF)


def body(
    image,
    gain_attn,
    w_qkv_fine,
    scale_fine,
    w_out_fine,
    gain_ffn,
    w_ffn_in,
    w_ffn_out,
    w_merge,
    gain_coarse,
    w_qkv_coarse,
    scale_coarse,
    w_out_coarse,
):
    vmem = pl.BlockSpec(memory_space=pltpu.VMEM)
    smem = pl.BlockSpec(memory_space=pltpu.SMEM)
    hbm = pl.BlockSpec(memory_space=pl.ANY)
    dma = pltpu.SemaphoreType.DMA
    weights = (w_qkv_fine, w_out_fine, w_ffn_in, w_ffn_out, w_merge, w_qkv_coarse, w_out_coarse)
    fine_out, coarse_out = pl.pallas_call(
        kernel,
        out_shape=(pltpu.VMEM((FR * FC, FD), BF), pltpu.VMEM((CT, CD), BF)),
        in_specs=[hbm, vmem, hbm, smem, hbm, vmem, hbm, hbm, hbm, vmem, hbm, smem, hbm],
        out_specs=(vmem, vmem),
        scratch_shapes=[
            pltpu.VMEM((PR, FC, FD), BF),
            pltpu.VMEM((64, FD), BF),
            pltpu.VMEM((2, 64, FD), BF),
            pltpu.VMEM((FR * FC, FD), BF),
            pltpu.VMEM((PR, FC, FD), BF),
            pltpu.VMEM((PR, FC, FD), BF),
            pltpu.VMEM((SIDE, FD), BF),
            pltpu.VMEM((SIDE, FD), BF),
            pltpu.VMEM((8 * FC, WINDOW), F32),
            pltpu.VMEM((8 * FC, SIDE), jnp.int32),
            pltpu.VMEM((FR * FC, FD), BF),
            pltpu.VMEM((CT, CD), BF),
            pltpu.VMEM((CT, CD), BF),
            pltpu.VMEM((2, NHEAD, HT + HEAD // 2, 128), BF),
            pltpu.VMEM((NHEAD, HT + HEAD // 2, 128), BF),
            pltpu.VMEM((NBLOCK, BLOCK, 128), BF),
            pltpu.VMEM((NHEAD, HEAD // 2, 128), BF),
            pltpu.VMEM((128, QUERIES), BF),
            pltpu.VMEM((HEAD + 8, QUERIES), F32),
            pltpu.VMEM((NHEAD, HEAD, CT), BF),
            pltpu.VMEM((NHEAD, HEAD, CT), BF),
        ]
        + [pltpu.VMEM(w.shape, BF) for w in weights]
        + [dma((8,)), dma((8,)), dma((8,))]
        + [dma((3, 16))] * 2
        + [dma((16,))] * 4,
        compiler_params=pltpu.CompilerParams(
            collective_id=0, has_side_effects=True, vmem_limit_bytes=VMEM_LIMIT
        ),
        name="window",
    )(
        image,
        gain_attn.reshape(1, -1),
        w_qkv_fine,
        scale_fine.reshape(1, -1),
        w_out_fine,
        gain_ffn.reshape(1, -1),
        w_ffn_in,
        w_ffn_out,
        w_merge,
        gain_coarse.reshape(1, -1),
        w_qkv_coarse,
        scale_coarse.reshape(1, -1),
        w_out_coarse,
    )
    return fine_out.reshape(image.shape), coarse_out.reshape(FR // 2, FC // 2, CD)


def solution(mesh):
    placed = (P("rows", "seq", None),) + (P(),) * 12
    return jax.shard_map(
        body,
        mesh=mesh,
        in_specs=placed,
        out_specs=(P("rows", "seq", None), P("rows", "seq", None)),
        check_vma=False,
    )
```

time: 78.2 us -> 74.3 us (0.950)
  Pallas kernels: 75.3 us -> 71.4 us
    pallas_call x1, Pallas kernels: 75.3 us -> 71.4 us  [body(): pl.pallas_call(kernel, out_shape=(pltpu.VMEM((FR * FC, FD), BF), pltpu.VM...]
where the time goes in v3:
time: 74.3 us; the launch traced here: 73.4 us
  Pallas kernels  71.4 us (96%)
  local copies, waits for them, and re-layouts  1.41 us (2%)
    pallas_call x1, Pallas kernels, body(): pl.pallas_call(kernel, out_shape=(pltpu.VMEM((FR * FC, FD), BF), pltpu.VM...  71.4 us

profile of v3, /device:TPU:1, one launch (start us, length us, event | category | flops | bytes accessed | tf_op | source)
XLA Modules:
  0.0 73.4 jit_solution(2664579005419510092)
XLA Ops:
  0.6 71.4 %window.1 = (bf16[512,256]{1,0:T(8,128)(2,1)S(1)}, bf16[128,1024]{1,0:T(8,128)(2,1)S(1)}) custom-call(bf16[8,64,256]{2,1,0:T(8,128)(2,1)} %image.1, f32[1,256]{1,0:T(1,128)} %bitcast.10, bf16[256,768]{1,0:T(8,128)(2,1)} %w_qkv_hbm.1, f32[1,4]{1,0:T(1,128)} %bitcast.12, bf16[256,256]{1,0:T(8,128)(2,1)} %w_proj_hbm.1, f32[1,256]{1,0:T(1,128)} %bitcast.11, ...), custom_call_target="tpu_custom_call" | custom-call | tf_op jit(solution)/shard_map/window/pallas_call | solution.py:524
  72.0 0.7 copy.17
  72.7 0.7 copy.18

commit v4 on v3

--- a/solution.py
+++ b/solution.py
@@ -303,38 +303,40 @@
         coarse_in[tokens, :] = coarse
         normed = rms(coarse.astype(F32), gain_coarse[...])
 
-        def heads(which, dy):
-            start = which * CD + lax.rem(y + dy, 4) * 256
-            cols = pl.ds(pl.multiple_of(start, 256), 256)
+        def heads(which):
+            cols = slice(which * CD, (which + 1) * CD)
             return dot(normed, w_coarse[:, cols]).astype(BF).astype(F32)
 
-        def query_part(n, dy):
-            query = unit(heads(0, dy), blocks)
-            for j in range(2):
-                pair = query[:, j * 128 : (j + 1) * 128]
+        def unit_groups(values):
+            return [unit(values[:, c : c + 256], blocks) for c in range(0, CD, 256)]
+
+        def query_part():
+            query = unit_groups(heads(0))
+            for p in range(8):
+                pair = query[p // 2][:, (p % 2) * 128 : (p % 2 + 1) * 128]
                 turned = jnp.concatenate([pair, pair], axis=0).T
                 for e in range(2):
                     first, second = turned[e * 64 : e * 64 + 32], turned[e * 64 + 32 : e * 64 + 64]
                     part = jnp.where(low_half[:32], first, second).astype(BF)
-                    messages[t, n * 4 + 2 * j + e, HT:] = part
-
-        def key_part(n, dy):
-            key = unit(heads(1, dy), blocks)
-            value = heads(2, dy)
-            for j in range(2):
-                k2 = key[:, j * 128 : (j + 1) * 128]
-                v2 = value[:, j * 128 : (j + 1) * 128]
+                    messages[t, 2 * p + e, HT:] = part
+
+        def key_part():
+            key = unit_groups(heads(1))
+            value = heads(2)
+            for p in range(8):
+                k2 = key[p // 2][:, (p % 2) * 128 : (p % 2 + 1) * 128]
+                v2 = value[:, p * 128 : (p + 1) * 128]
                 even = jnp.where(low_half, k2, pltpu.roll(v2, HEAD, 1))
                 odd = jnp.where(low_half, pltpu.roll(k2, HEAD, 1), v2)
-                messages[t, n * 4 + 2 * j, :HT] = even.astype(BF)
-                messages[t, n * 4 + 2 * j + 1, :HT] = odd.astype(BF)
-
-        def send(n, dy, name, rows_here, target):
-            for dz in range(4):
-                k = n * 4 + dz
+                messages[t, 2 * p, :HT] = even.astype(BF)
+                messages[t, 2 * p + 1, :HT] = odd.astype(BF)
+
+        def send(name, rows_here, target):
+            for k, (dy, dz) in enumerate(partners):
                 if k != own:
+                    their_head = lax.rem(y + dy, 4) * 4 + lax.rem(z + dz, 4)
                     copies[name, k] = remote(
-                        messages.at[t, n * 4 + lax.rem(z + dz, 4), rows_here],
+                        messages.at[t, their_head, rows_here],
                         target(k),
                         x_send.at[name, k],
                         x_recv.at[name, k],
@@ -343,18 +345,15 @@
                     copies[name, k].start()
 
         if t == 0:
-            for n, dy in enumerate(ORDER):
-                query_part(n, dy)
-                key_part(n, dy)
-                send(n, dy, 0, pl.ds(0, 96), lambda k: landed.at[k])
+            query_part()
+            key_part()
+            send(0, pl.ds(0, 96), lambda k: landed.at[k])
         else:
-            for n, dy in enumerate(ORDER):
-                query_part(n, dy)
-                send(n, dy, 1, pl.ds(HT, 32), lambda k: q_buf.at[k])
-            for n, dy in enumerate(ORDER):
-                key_part(n, dy)
-                send(n, dy, 2, pl.ds(0, HT), lambda k: kv_buf.at[2, pl.ds(k * HT, HT)])
-            kv_buf[2, own * HT : (own + 1) * HT, :] = messages[1, own + z, :HT]
+            query_part()
+            send(1, pl.ds(HT, 32), lambda k: q_buf.at[k])
+            key_part()
+            send(2, pl.ds(0, HT), lambda k: kv_buf.at[2, pl.ds(k * HT, HT)])
+            kv_buf[2, own * HT : (own + 1) * HT, :] = messages[1, head, :HT]
 
     for place in halo:
         if place != (1, 0) and place != (-1, 0):
@@ -420,69 +419,100 @@
                 copies[k].wait()
         if b == 0:
             for k in range(16):
-                part = messages[0, own + z, :HT] if k == own else landed[k, :HT]
+                part = messages[0, head, :HT] if k == own else landed[k, :HT]
                 kv_buf[0, k * HT : (k + 1) * HT, :] = part
         for target in start_after.get(b, ()):
             gathers[target].start()
 
-    arrivals(0)
-    for k in range(16):
-        if k == own:
-            parts = [messages[t, own + z, HT:] for t in range(2)]
-        else:
-            copies[1, k].wait()
-            parts = [landed[k, HT:], q_buf[k]]
-        parts = [part.astype(F32) for part in parts]
-        top = jnp.where(low_half[:32], parts[0], pltpu.roll(parts[1], HEAD, 1))
-        end = jnp.where(low_half[:32], pltpu.roll(parts[0], HEAD, 1), parts[1])
-        q_full[0:HEAD, k * CT : (k + 1) * CT] = jnp.concatenate([top, end], axis=0).astype(BF)
-
+    def assemble(t):
+        for k in range(0, 16, 2):
+            parts = []
+            for j in (k, k + 1):
+                if j == own:
+                    part = messages[t, head, HT:]
+                elif t == 0:
+                    part = landed[j, HT:]
+                else:
+                    copies[1, j].wait()
+                    part = q_buf[j]
+                parts.append(part.astype(F32))
+            top = jnp.where(low_half[:32], parts[0], pltpu.roll(parts[1], HEAD, 1))
+            end = jnp.where(low_half[:32], pltpu.roll(parts[0], HEAD, 1), parts[1])
+            cols = slice(t * half + k * HT, t * half + (k + 2) * HT)
+            q_full[0:HEAD, cols] = jnp.concatenate([top, end], axis=0).astype(BF)
+
+    o_copies = {}
+    half, quarter = QUERIES // 2, QUERIES // 4
     head_factor = scale_coarse[0, head] * (LOG2E / HEAD)
     ones = jnp.ones((8, BLOCK), BF)
-    half = QUERIES // 2
-
-    def process(b, halves):
+
+    def process(b, parts):
         kv = kv_buf[b]
         lhs = jnp.concatenate([kv.T[HEAD:], ones], axis=0)
-        for u in halves:
-            cols = slice(u * half, (u + 1) * half)
+        for cols in parts:
             weights = jnp.exp2(dot(kv, q_full[:, cols]) * head_factor).astype(BF)
             acc[:, cols] += dot(lhs, weights)
 
-    def step(b, carry):
-        for block in sorted(arrive):
-            if 0 < block < 12:
-                pl.when(b == block)(lambda block=block: arrivals(block))
-        process(b, (0, 1))
+    all_parts = [slice(i * quarter, (i + 1) * quarter) for i in range(4)]
+
+    arrivals(0)
+    assemble(0)
+    process(0, all_parts[:2])
+    arrivals(1)
+    process(1, all_parts[:2])
+    assemble(1)
+
+    def step(i, carry):
+        @pl.when(i < 2)
+        def _():
+            process(i, all_parts[2:])
+
+        @pl.when(i >= 2)
+        def _():
+            for block in sorted(arrive):
+                if 1 < block < 12:
+                    pl.when(i == block)(lambda block=block: arrivals(block))
+            process(i, [slice(0, half), slice(half, QUERIES)])
+
         return carry
 
     lax.fori_loop(0, 12, step, 0)
 
-    o_copies = {}
-    for u in range(2):
-
-        def last(b, carry):
-            if u == 0:
-                for block in (12, 14, 15):
-                    pl.when(b == block)(lambda block=block: arrivals(block))
-            process(b, (u,))
+    low_rows = lax.broadcasted_iota(jnp.int32, (HEAD, 128), 1) < HEAD
+    for first in (0, 1):
+        parts = [all_parts[first], all_parts[first + 2]]
+
+        def last(i, carry):
+            if first == 0:
+                pl.when(i == 0)(lambda: arrivals(12))
+
+                @pl.when(i == 2)
+                def _():
+                    arrivals(14)
+                    arrivals(15)
+
+            process(12 + i, parts)
             return carry
 
-        lax.fori_loop(12, NBLOCK, last, 0)
-        cols = slice(u * half, (u + 1) * half)
-        inverse = 1.0 / acc[HEAD : HEAD + 1, cols]
-        done = (acc[0:HEAD, cols] * inverse).astype(BF)
-        for k in range(u * 8, u * 8 + 8):
-            dy, dz = partners[k]
-            part = done[:, (k % 8) * CT : (k % 8 + 1) * CT]
-            if k == own:
-                back[head] = part
-                continue
-            o_buf[k] = part
-            o_copies[k] = remote(
-                o_buf.at[k], back.at[head], o_send.at[k], o_recv.at[k], at(-dy, -dz)
+        lax.fori_loop(0, 4, last, 0)
+        done = [acc[0:HEAD, cols] * (1.0 / acc[HEAD : HEAD + 1, cols]) for cols in parts]
+        for k in range(first * 8, first * 8 + 8, 2):
+            start = (k - first * 8) * HT
+            early, late = (half_done[:, start : start + 128] for half_done in done)
+            both = (
+                jnp.where(low_rows, early, pltpu.roll(late, HEAD, 1)).astype(BF),
+                jnp.where(low_rows, pltpu.roll(early, HEAD, 1), late).astype(BF),
             )
-            o_copies[k].start()
+            for j in (k, k + 1):
+                if j == own:
+                    back[head] = both[j - k]
+                    continue
+                dy, dz = partners[j]
+                o_buf[j] = both[j - k]
+                o_copies[j] = remote(
+                    o_buf.at[j], back.at[head], o_send.at[j], o_recv.at[j], at(-dy, -dz)
+                )
+                o_copies[j].start()
 
     for copy in gathers.values():
         copy.wait_send()

time: 74.3 us -> 72.7 us (0.978); the launches traced: 73.4 us -> 72.6 us
  Pallas kernels: 71.4 us -> 70.5 us
    pallas_call x1, Pallas kernels: 71.4 us -> 70.5 us  [body(): pl.pallas_call(kernel, out_shape=(pltpu.VMEM((FR * FC, FD), BF), pltpu.VM...]
where the time goes in v4:
time: 72.7 us; the launch traced here: 72.6 us
  Pallas kernels  70.5 us (97%)
  local copies, waits for them, and re-layouts  1.41 us (2%)
    pallas_call x1, Pallas kernels, body(): pl.pallas_call(kernel, out_shape=(pltpu.VMEM((FR * FC, FD), BF), pltpu.VM...  70.5 us

profile of v4, /device:TPU:1, one launch (start us, length us, event | category | flops | bytes accessed | tf_op | source)
XLA Modules:
  0.0 72.6 jit_solution(1517113206063216193)
XLA Ops:
  0.6 70.5 %window.1 = (bf16[512,256]{1,0:T(8,128)(2,1)S(1)}, bf16[128,1024]{1,0:T(8,128)(2,1)S(1)}) custom-call(bf16[8,64,256]{2,1,0:T(8,128)(2,1)} %image.1, f32[1,256]{1,0:T(1,128)} %bitcast.10, bf16[256,768]{1,0:T(8,128)(2,1)} %w_qkv_hbm.1, f32[1,4]{1,0:T(1,128)} %bitcast.12, bf16[256,256]{1,0:T(8,128)(2,1)} %w_proj_hbm.1, f32[1,256]{1,0:T(1,128)} %bitcast.11, ...), custom_call_target="tpu_custom_call" | custom-call | tf_op jit(solution)/shard_map/window/pallas_call | solution.py:554
  71.2 0.7 copy.17
  71.9 0.7 copy.18

commit v5 on v4

--- a/solution.py
+++ b/solution.py
@@ -15,8 +15,9 @@
 
 FR, FC, FD = 8, 64, 256
 PR = FR + 6
-WINDOW = 8 * FC
+OWN = FR * FC
 SIDE = 128
+HALO = SIDE + 3 * FC
 CT, CD = 128, 1024
 NHEAD = 16
 HT = CT // 2
@@ -45,30 +46,32 @@
 
 def kernel(
     image,
-    gain_attn,
+    gain_attn_hbm,
     w_qkv_hbm,
-    scale_fine,
+    scale_fine_hbm,
     w_proj_hbm,
-    gain_ffn,
+    gain_ffn_hbm,
     w_in_hbm,
     w_ffn_hbm,
     w_merge_hbm,
-    gain_coarse,
+    gain_coarse_hbm,
     w_coarse_hbm,
-    scale_coarse,
+    scale_coarse_hbm,
     w_out_hbm,
     fine_out,
     out,
     xpad,
     packed,
     side,
-    queries,
     keys,
     vals,
-    side_keys,
-    side_vals,
+    halo_keys,
+    halo_vals,
     bias,
-    side_gap,
+    halo_gap,
+    stacked,
+    own_total,
+    own_sum,
     attended,
     merged,
     coarse_in,
@@ -87,6 +90,11 @@
     w_merge,
     w_coarse,
     w_out,
+    gain_attn,
+    gain_ffn,
+    gain_coarse,
+    scale_fine,
+    scale_coarse,
     load_sem,
     halo_send,
     halo_recv,
@@ -118,6 +126,12 @@
     partners = [(dy, dz) for dy in ORDER for dz in range(4)]
     own = partners.index((0, 0))
 
+    def load(source, target, i):
+        copy = pltpu.make_async_copy(source, target, load_sem.at[i])
+        copy.start()
+        return copy
+
+    image_load = load(image, xpad.at[pl.ds(3, FR)], 0)
     barrier = pltpu.get_barrier_semaphore()
     everyone = [beside(dr, ds) for dr, ds in around]
     everyone += [at(dy, dz) for k, (dy, dz) in enumerate(partners) if k != own]
@@ -125,13 +139,14 @@
     for there in everyone:
         pl.semaphore_signal(barrier, inc=1, device_id=there, device_id_type=MESH)
 
-    def load(source, target, i):
-        copy = pltpu.make_async_copy(source, target, load_sem.at[i])
-        copy.start()
-        return copy
-
-    image_load = load(image, xpad.at[pl.ds(3, FR)], 0)
     w_qkv_load = load(w_qkv_hbm, w_qkv, 1)
+    small_loads = [
+        load(gain_attn_hbm, gain_attn, 8),
+        load(gain_ffn_hbm, gain_ffn, 9),
+        load(gain_coarse_hbm, gain_coarse, 10),
+        load(scale_fine_hbm, scale_fine, 11),
+        load(scale_coarse_hbm, scale_coarse, 12),
+    ]
     w_proj_load = load(w_proj_hbm, w_proj, 2)
     w_in_load = load(w_in_hbm, w_in, 3)
     w_ffn_load = load(w_ffn_hbm, w_ffn, 4)
@@ -159,7 +174,6 @@
         halo[place] = remote(source, target, halo_send.at[i], halo_recv.at[i], beside(*place))
         halo[place].start()
 
-    send_halo((-1, 0), xpad.at[pl.ds(3, 3)], xpad.at[pl.ds(FR + 3, 3)])
     send_halo((1, 0), xpad.at[pl.ds(FR, 3)], xpad.at[pl.ds(0, 3)])
     take = lax.broadcasted_iota(jnp.int32, (64, FR * FC), 0)
     come = lax.broadcasted_iota(jnp.int32, (64, FR * FC), 1)
@@ -171,13 +185,16 @@
         send_halo((0, ds), packed.at[pl.ds(start, 32)], side.at[there, pl.ds(16, 32)])
         send_halo((-1, ds), packed.at[pl.ds(start, 16)], side.at[there, pl.ds(48, 16)])
         send_halo((1, ds), packed.at[pl.ds(start + 16, 16)], side.at[there, pl.ds(0, 16)])
+    send_halo((-1, 0), xpad.at[pl.ds(3, 3)], xpad.at[pl.ds(FR + 3, 3)])
 
     group = (lax.broadcasted_iota(jnp.int32, (FD, FD), 0) >> 6) == (
         lax.broadcasted_iota(jnp.int32, (FD, FD), 1) >> 6
     )
     blocks = jnp.where(group, 1.0 / HEAD, 0.0).astype(BF)
+    w_qkv_load.wait()
+    for copy in small_loads:
+        copy.wait()
     gain = gain_attn[...]
-    w_qkv_load.wait()
 
     def project(tokens, first):
         normed = rms(tokens.astype(F32), gain)
@@ -186,74 +203,84 @@
     def unit_bf(values):
         return unit(values.astype(F32), blocks).astype(BF)
 
+    lane_head = lax.broadcasted_iota(jnp.int32, (FC, FD), 1) >> 6
     for i in range(2):
-        rows_here = slice(3 + 4 * i, 7 + 4 * i)
-        triple = project(xpad[rows_here].reshape(4 * FC, FD), 0)
-        queries[i * 4 * FC : (i + 1) * 4 * FC, :] = unit_bf(triple[:, :FD])
-        keys[rows_here] = unit_bf(triple[:, FD : 2 * FD]).reshape(4, FC, FD)
-        vals[rows_here] = triple[:, 2 * FD :].reshape(4, FC, FD)
-
-    gap = lax.broadcasted_iota(jnp.int32, (FC, FC), 1) - lax.broadcasted_iota(
-        jnp.int32, (FC, FC), 0
+        tokens = slice(i * 256, (i + 1) * 256)
+        triple = project(xpad[3 + 4 * i : 7 + 4 * i].reshape(256, FD), 0)
+        query = unit(triple[:, :FD].astype(F32), blocks)
+        for r in range(4):
+            for h in range(4):
+                one = jnp.where(lane_head == h, query[r * FC : (r + 1) * FC], 0.0)
+                start = ((r % 2) * 4 + h) * FC
+                stacked[i * 2 + r // 2, start : start + FC, :] = one.astype(BF)
+        keys[tokens, :] = unit_bf(triple[:, FD : 2 * FD])
+        vals[tokens, :] = triple[:, 2 * FD :]
+
+    query_col = lax.broadcasted_iota(jnp.int32, (FC, OWN), 0)
+    gap = (lax.broadcasted_iota(jnp.int32, (FC, OWN), 1) & 63) - query_col
+    near = jnp.where((gap >= -3) & (gap <= 3), 0.0, -1e30).astype(F32)
+    bias[...] = jnp.concatenate([near] * 4, axis=0)
+    own_row = lax.broadcasted_iota(jnp.int32, (1, OWN), 1) >> 6
+    factor = jnp.concatenate(
+        [
+            jnp.broadcast_to(scale_fine[0:1, h : h + 1] * (LOG2E / HEAD), (FC, 1))
+            for h in range(4)
+        ],
+        axis=0,
     )
-    near = jnp.where((gap >= -3) & (gap <= 3), 0.0, -1e30).astype(F32)
-    never = jnp.full((FC, FC), -1e30, F32)
-    query_col = lax.broadcasted_iota(jnp.int32, (FC, SIDE), 0)
-    slot = lax.broadcasted_iota(jnp.int32, (FC, SIDE), 1)
+    factors = jnp.concatenate([factor, factor], axis=0)
+    last_dims = (((1,), (1,)), ((), ()))
+
+    def attend_own(i):
+        scores = lax.dot_general(
+            stacked[i], keys[...], last_dims, preferred_element_type=F32
+        )
+        weights = []
+        for r in range(2):
+            off = own_row + 3 - r - 2 * i
+            row_bias = jnp.where((off >= 0) & (off <= 6), 0.0, -1e30).astype(F32)
+            part = scores[r * 256 : (r + 1) * 256] * factor + (bias[...] + row_bias)
+            weights.append(jnp.exp2(part))
+        weights = jnp.concatenate(weights, axis=0)
+        own_total[i] = dot(weights.astype(BF), vals[...])
+        weight_sum = weights[:, :128]
+        for j in range(128, OWN, 128):
+            weight_sum = weight_sum + weights[:, j : j + 128]
+        own_sum[i] = weight_sum
+
+    query_col = lax.broadcasted_iota(jnp.int32, (FC, HALO), 0)
+    slot = lax.broadcasted_iota(jnp.int32, (FC, HALO), 1)
+    beyond = slot - SIDE
     right = slot >> 6
-    side_row = ((slot & 63) >> 2) - 1
-    side_col = (slot & 3) - 4 + right * (FC + 4)
-    side_global = row * FR + side_row - 3
-    side_near = (side_col - query_col >= -3) & (side_col - query_col <= 3)
-    side_near = side_near & (side_global >= 0) & (side_global < n_rows * FR)
-    side_near = side_near & ((right > 0) | (seq > 0)) & ((right < 1) | (seq < n_seq - 1))
-    for r in range(2):
-        one = jnp.concatenate([near if r <= j <= r + 6 else never for j in range(8)], axis=1)
-        gap_row = jnp.where(side_near, side_row - r, 1000)
-        for h in range(4):
-            start = (r * 4 + h) * FC
-            bias[start : start + FC, :] = one
-            side_gap[start : start + FC, :] = gap_row
-
-    lane_head = lax.broadcasted_iota(jnp.int32, (FC, FD), 1) >> 6
-    factor = jnp.concatenate(
-        [jnp.full((FC, 1), scale_fine[0, h] * (LOG2E / HEAD), F32) for h in range(4)] * 2, axis=0
-    )
-    window_row = lax.broadcasted_iota(jnp.int32, (1, WINDOW), 1) >> 6
-    last_dims = (((1,), (1,)), ((), ()))
+    for t in range(2):
+        key_row = jnp.where(slot < SIDE, ((slot & 63) >> 2) - 1, (beyond >> 6) + t * (FR + 3))
+        key_col = jnp.where(slot < SIDE, (slot & 3) - 4 + right * (FC + 4), beyond & 63)
+        global_row = row * FR + key_row - 3
+        global_col = seq * FC + key_col
+        inside = (global_row >= 0) & (global_row < n_rows * FR)
+        inside = inside & (global_col >= 0) & (global_col < n_seq * FC)
+        inside = inside & (key_col - query_col >= -3) & (key_col - query_col <= 3)
+        gap = jnp.where(inside, key_row, 1000)
+        for r in range(2):
+            for h in range(4):
+                start = (r * 4 + h) * FC
+                halo_gap[t, start : start + FC, :] = gap - r
+
+    for i in range(4):
+        attend_own(i)
 
     def attend(i):
-        query = queries[i * 128 : (i + 1) * 128, :].astype(F32)
-        stacked = jnp.concatenate(
-            [
-                jnp.where(lane_head == h, query[r * FC : (r + 1) * FC], 0.0).astype(BF)
-                for r in range(2)
-                for h in range(4)
-            ],
-            axis=0,
+        t = i // 2
+        scores = lax.dot_general(
+            stacked[i], halo_keys[t], last_dims, preferred_element_type=F32
         )
-        window = slice(i * 2, i * 2 + 8)
-        scores = lax.dot_general(
-            stacked, keys[window].reshape(WINDOW, FD), last_dims, preferred_element_type=F32
+        off = halo_gap[t] - i * 2
+        weights = jnp.where((off >= 0) & (off <= 6), jnp.exp2(scores * factors), 0.0)
+        total = own_total[i] + dot(weights.astype(BF), halo_vals[t])
+        weight_sum = jnp.sum(own_sum[i], axis=-1, keepdims=True) + jnp.sum(
+            weights, axis=-1, keepdims=True
         )
-        side_scores = lax.dot_general(
-            stacked, side_keys[...], last_dims, preferred_element_type=F32
-        )
-        global_row = row * FR + i * 2 + window_row - 3
-        outside = (global_row < 0) | (global_row >= n_rows * FR)
-        key_bias = jnp.where(outside, -1e30, 0.0).astype(F32)
-        weights = jnp.exp2(scores * factor + (bias[...] + key_bias))
-        off = side_gap[...] - i * 2
-        side_weights = jnp.where(
-            (off >= 0) & (off <= 6), jnp.exp2(side_scores * factor), 0.0
-        )
-        total = dot(weights.astype(BF), vals[window].reshape(WINDOW, FD)) + dot(
-            side_weights.astype(BF), side_vals[...]
-        )
-        weight_sum = side_weights
-        for j in range(0, WINDOW, 128):
-            weight_sum = weight_sum + weights[:, j : j + 128]
-        scaled = total * (1.0 / jnp.sum(weight_sum, axis=-1, keepdims=True))
+        scaled = total * (1.0 / weight_sum)
         picked = []
         for r in range(2):
             parts = [scaled[(r * 4 + h) * FC : (r * 4 + h + 1) * FC] for h in range(4)]
@@ -263,10 +290,10 @@
             picked.append(merged_heads)
         attended[i * 128 : (i + 1) * 128, :] = jnp.concatenate(picked, axis=0).astype(BF)
 
-    def end_rows(rows_here):
+    def end_rows(t, rows_here):
         kv = project(xpad[rows_here].reshape(3 * FC, FD), FD)
-        keys[rows_here] = unit_bf(kv[:, :FD]).reshape(3, FC, FD)
-        vals[rows_here] = kv[:, FD:].reshape(3, FC, FD)
+        halo_keys[t, SIDE:, :] = unit_bf(kv[:, :FD])
+        halo_vals[t, SIDE:, :] = kv[:, FD:]
 
     hidden = w_ffn.shape[0]
     take = lax.broadcasted_iota(jnp.int32, (128, 128), 0)
@@ -359,10 +386,12 @@
         if place != (1, 0) and place != (-1, 0):
             halo[place].wait()
     side_kv = project(side[...].reshape(SIDE, FD), FD)
-    side_keys[...] = unit_bf(side_kv[:, :FD])
-    side_vals[...] = side_kv[:, FD:]
+    side_keys = unit_bf(side_kv[:, :FD])
+    for t in range(2):
+        halo_keys[t, :SIDE, :] = side_keys
+        halo_vals[t, :SIDE, :] = side_kv[:, FD:]
     halo[1, 0].wait()
-    end_rows(slice(0, 3))
+    end_rows(0, slice(0, 3))
     attend(0)
     attend(1)
     w_proj_load.wait()
@@ -373,7 +402,7 @@
     w_coarse_load.wait()
     exchange(0)
     halo[-1, 0].wait()
-    end_rows(slice(FR + 3, FR + 6))
+    end_rows(1, slice(FR + 3, FR + 6))
     attend(2)
     attend(3)
     feed(1)
@@ -443,7 +472,9 @@
 
     o_copies = {}
     half, quarter = QUERIES // 2, QUERIES // 4
-    head_factor = scale_coarse[0, head] * (LOG2E / HEAD)
+    of_head = lax.broadcasted_iota(jnp.int32, (1, NHEAD), 1) == head
+    head_scale = jnp.sum(jnp.where(of_head, scale_coarse[...], 0.0), axis=1, keepdims=True)
+    head_factor = head_scale * (LOG2E / HEAD)
     ones = jnp.ones((8, BLOCK), BF)
 
     def process(b, parts):
@@ -547,26 +578,27 @@
     w_out_coarse,
 ):
     vmem = pl.BlockSpec(memory_space=pltpu.VMEM)
-    smem = pl.BlockSpec(memory_space=pltpu.SMEM)
     hbm = pl.BlockSpec(memory_space=pl.ANY)
     dma = pltpu.SemaphoreType.DMA
     weights = (w_qkv_fine, w_out_fine, w_ffn_in, w_ffn_out, w_merge, w_qkv_coarse, w_out_coarse)
     fine_out, coarse_out = pl.pallas_call(
         kernel,
         out_shape=(pltpu.VMEM((FR * FC, FD), BF), pltpu.VMEM((CT, CD), BF)),
-        in_specs=[hbm, vmem, hbm, smem, hbm, vmem, hbm, hbm, hbm, vmem, hbm, smem, hbm],
+        in_specs=[hbm] * 13,
         out_specs=(vmem, vmem),
         scratch_shapes=[
             pltpu.VMEM((PR, FC, FD), BF),
             pltpu.VMEM((64, FD), BF),
             pltpu.VMEM((2, 64, FD), BF),
-            pltpu.VMEM((FR * FC, FD), BF),
-            pltpu.VMEM((PR, FC, FD), BF),
-            pltpu.VMEM((PR, FC, FD), BF),
-            pltpu.VMEM((SIDE, FD), BF),
-            pltpu.VMEM((SIDE, FD), BF),
-            pltpu.VMEM((8 * FC, WINDOW), F32),
-            pltpu.VMEM((8 * FC, SIDE), jnp.int32),
+            pltpu.VMEM((OWN, FD), BF),
+            pltpu.VMEM((OWN, FD), BF),
+            pltpu.VMEM((2, HALO, FD), BF),
+            pltpu.VMEM((2, HALO, FD), BF),
+            pltpu.VMEM((4 * FC, OWN), F32),
+            pltpu.VMEM((2, 8 * FC, HALO), jnp.int32),
+            pltpu.VMEM((4, 8 * FC, FD), BF),
+            pltpu.VMEM((4, 8 * FC, FD), F32),
+            pltpu.VMEM((4, 8 * FC, 128), F32),
             pltpu.VMEM((FR * FC, FD), BF),
             pltpu.VMEM((CT, CD), BF),
             pltpu.VMEM((CT, CD), BF),
@@ -580,7 +612,8 @@
             pltpu.VMEM((NHEAD, HEAD, CT), BF),
         ]
         + [pltpu.VMEM(w.shape, BF) for w in weights]
-        + [dma((8,)), dma((8,)), dma((8,))]
+        + [pltpu.VMEM((1, n), F32) for n in (FD, FD, CD, 4, NHEAD)]
+        + [dma((13,)), dma((8,)), dma((8,))]
         + [dma((3, 16))] * 2
         + [dma((16,))] * 4,
         compiler_params=pltpu.CompilerParams(

time: 72.7 us -> 71.8 us (0.988)
  Pallas kernels: 70.5 us -> 69.6 us
    pallas_call x1, Pallas kernels: 70.5 us -> 69.6 us  [body(): pl.pallas_call(kernel, out_shape=(pltpu.VMEM((FR * FC, FD), BF), pltpu.VM...]
where the time goes in v5:
time: 71.8 us; the launch traced here: 71.6 us
  Pallas kernels  69.6 us (97%)
  local copies, waits for them, and re-layouts  1.41 us (2%)
    pallas_call x1, Pallas kernels, body(): pl.pallas_call(kernel, out_shape=(pltpu.VMEM((FR * FC, FD), BF), pltpu.VM...  69.6 us

profile of v5, /device:TPU:1, one launch (start us, length us, event | category | flops | bytes accessed | tf_op | source)
XLA Modules:
  0.0 71.6 jit_solution(9752961117484206821)
XLA Ops:
  0.6 69.6 %window.1 = (bf16[512,256]{1,0:T(8,128)(2,1)S(1)}, bf16[128,1024]{1,0:T(8,128)(2,1)S(1)}) custom-call(bf16[8,64,256]{2,1,0:T(8,128)(2,1)} %image.1, f32[1,256]{1,0:T(1,128)} %bitcast.10, bf16[256,768]{1,0:T(8,128)(2,1)} %w_qkv_hbm.1, f32[1,4]{1,0:T(1,128)} %bitcast.12, bf16[256,256]{1,0:T(8,128)(2,1)} %w_proj_hbm.1, f32[1,256]{1,0:T(1,128)} %bitcast.11, ...), custom_call_target="tpu_custom_call" | custom-call | tf_op jit(solution)/shard_map/window/pallas_call | solution.py:584
  70.2 0.7 copy.17
  70.9 0.7 copy.18

commit v6 on v5

--- a/solution.py
+++ b/solution.py
@@ -125,6 +125,9 @@
     around = [(dr, ds) for dr in (0, -1, 1) for ds in (0, -1, 1) if (dr, ds) != (0, 0)]
     partners = [(dy, dz) for dy in ORDER for dz in range(4)]
     own = partners.index((0, 0))
+    hops = (0, 1, 2, 1)
+    farthest = sorted(range(16), key=lambda k: -hops[partners[k][0]] - hops[partners[k][1]])
+    farthest.remove(own)
 
     def load(source, target, i):
         copy = pltpu.make_async_copy(source, target, load_sem.at[i])
@@ -359,17 +362,17 @@
                 messages[t, 2 * p + 1, :HT] = odd.astype(BF)
 
         def send(name, rows_here, target):
-            for k, (dy, dz) in enumerate(partners):
-                if k != own:
-                    their_head = lax.rem(y + dy, 4) * 4 + lax.rem(z + dz, 4)
-                    copies[name, k] = remote(
-                        messages.at[t, their_head, rows_here],
-                        target(k),
-                        x_send.at[name, k],
-                        x_recv.at[name, k],
-                        at(dy, dz),
-                    )
-                    copies[name, k].start()
+            for k in farthest:
+                dy, dz = partners[k]
+                their_head = lax.rem(y + dy, 4) * 4 + lax.rem(z + dz, 4)
+                copies[name, k] = remote(
+                    messages.at[t, their_head, rows_here],
+                    target(k),
+                    x_send.at[name, k],
+                    x_recv.at[name, k],
+                    at(dy, dz),
+                )
+                copies[name, k].start()
 
         if t == 0:
             query_part()
@@ -437,7 +440,7 @@
     arrive[8] = ("gather", (8, 9))
     arrive[12] = ("gather", (12, 13))
     del arrive[9], arrive[13]
-    start_after = {0: (4, 5, 1), 2: (8, 9, 3), 4: (12, 6), 5: (7,), 8: (13, 10, 11), 12: (14, 15)}
+    start_after = {0: (1, 4, 5), 2: (3, 8, 9), 4: (6, 12), 5: (7,), 8: (10, 11, 13), 12: (14, 15)}
 
     def arrivals(b):
         kind, which = arrive[b]

time: 71.8 us -> 70.3 us (0.979)
  Pallas kernels: 69.6 us -> 68.1 us
    pallas_call x1, Pallas kernels: 69.6 us -> 68.1 us  [body(): pl.pallas_call(kernel, out_shape=(pltpu.VMEM((FR * FC, FD), BF), pltpu.VM...]
where the time goes in v6:
time: 70.3 us; the launch traced here: 70.1 us
  Pallas kernels  68.1 us (97%)
  local copies, waits for them, and re-layouts  1.41 us (2%)
    pallas_call x1, Pallas kernels, body(): pl.pallas_call(kernel, out_shape=(pltpu.VMEM((FR * FC, FD), BF), pltpu.VM...  68.1 us
    unnamed x2, local copies, waits for them, and re-layouts  1.41 us

profile of v6, /device:TPU:1, one launch (start us, length us, event | category | flops | bytes accessed | tf_op | source)
XLA Modules:
  0.0 70.1 jit_solution(3424958001581735750)
XLA Ops:
  0.6 68.1 %window.1 = (bf16[512,256]{1,0:T(8,128)(2,1)S(1)}, bf16[128,1024]{1,0:T(8,128)(2,1)S(1)}) custom-call(bf16[8,64,256]{2,1,0:T(8,128)(2,1)} %image.1, f32[1,256]{1,0:T(1,128)} %bitcast.10, bf16[256,768]{1,0:T(8,128)(2,1)} %w_qkv_hbm.1, f32[1,4]{1,0:T(1,128)} %bitcast.12, bf16[256,256]{1,0:T(8,128)(2,1)} %w_proj_hbm.1, f32[1,256]{1,0:T(1,128)} %bitcast.11, ...), custom_call_target="tpu_custom_call" | custom-call | tf_op jit(solution)/shard_map/window/pallas_call | solution.py:587
  68.7 0.7 %copy.17 = bf16[8,64,256]{2,1,0:T(8,128)(2,1)} copy(bf16[8,64,256]{2,1,0:T(8,128)(2,1)S(1)} %bitcast.8) | data formatting | bytes 524288
  69.4 0.7 %copy.18 = bf16[4,32,1024]{2,1,0:T(8,128)(2,1)} copy(bf16[4,32,1024]{2,1,0:T(8,128)(2,1)S(1)} %bitcast.7) | data formatting | bytes 524288

commit v7 on v6

--- a/solution.py
+++ b/solution.py
@@ -541,8 +541,10 @@
                 if j == own:
                     back[head] = both[j - k]
                     continue
+                o_buf[j] = both[j - k]
+        for j in farthest:
+            if first * 8 <= j < first * 8 + 8:
                 dy, dz = partners[j]
-                o_buf[j] = both[j - k]
                 o_copies[j] = remote(
                     o_buf.at[j], back.at[head], o_send.at[j], o_recv.at[j], at(-dy, -dz)
                 )

time: 70.3 us -> 70.4 us (level)
  no operation moved by 1% of the time
where the time goes in v7:
time: 70.4 us; the launch traced here: 70.3 us
  Pallas kernels  68.2 us (97%)
  local copies, waits for them, and re-layouts  1.41 us (2%)
    pallas_call x1, Pallas kernels, body(): pl.pallas_call(kernel, out_shape=(pltpu.VMEM((FR * FC, FD), BF), pltpu.VM...  68.2 us

profile of v7, /device:TPU:1, one launch (start us, length us, event | category | flops | bytes accessed | tf_op | source)
XLA Modules:
  0.0 70.3 jit_solution(11231772244239450582)
XLA Ops:
  0.6 68.2 %window.1 = (bf16[512,256]{1,0:T(8,128)(2,1)S(1)}, bf16[128,1024]{1,0:T(8,128)(2,1)S(1)}) custom-call(bf16[8,64,256]{2,1,0:T(8,128)(2,1)} %image.1, f32[1,256]{1,0:T(1,128)} %bitcast.10, bf16[256,768]{1,0:T(8,128)(2,1)} %w_qkv_hbm.1, f32[1,4]{1,0:T(1,128)} %bitcast.12, bf16[256,256]{1,0:T(8,128)(2,1)} %w_proj_hbm.1, f32[1,256]{1,0:T(1,128)} %bitcast.11, ...), custom_call_target="tpu_custom_call" | custom-call | tf_op jit(solution)/shard_map/window/pallas_call | solution.py:589
  68.9 0.7 %copy.17 = bf16[8,64,256]{2,1,0:T(8,128)(2,1)} copy(bf16[8,64,256]{2,1,0:T(8,128)(2,1)S(1)} %bitcast.8) | data formatting | bytes 524288
  69.6 0.7 copy.18
